TPU v7x, 32 devices: a whole 2x2x4 slice. The times are simulated.
32 devices in a mesh: row: 4 (over y, x), col: 8 (over z, core).
Axes of the slice: x: 2, y: 2, z: 4, core: 2. Of those that a mesh axis runs over, the one named last changes fastest.
Arguments:
- bricks: bfloat16 [4, 8, 2, 16, 128, 128], P('row', 'col'), may hold values from -98304 to 98304
- brick_coords: int32 [4, 8, 3, 2], P('row', 'col'), may hold values from 0 to 31, as said below
- brick_counts: int32 [4, 8], P('row', 'col'), may hold values from 0 to 2, as said below
- step_sizes: float32 [2, 3], replicated, may hold values from 0.3 to 1
- init_a: float32 [4, 512, 256], P('row', 'col'), may hold values from -6 to 6
- init_b: float32 [8, 256, 256], P('col', 'row'), may hold values from -6 to 6
- init_c: float32 [512, 256], replicated, may hold values from -6 to 6
Outputs:
- factor_a: float32 [4, 512, 256], P('row', 'col')
- factor_b: float32 [8, 256, 256], P('col', 'row')
- factor_c: float32 [512, 256], replicated
Inputs may be any that keep to these rules, and one draw needn't show every extreme that they name: brick_counts of rows r and (r + half of the row axis) mod the row axis in one column add up to at most 3; some device holds 2 bricks. `brick_coords`: component 0 is below 4, component 1 below 2, component 2 below 32; dead slots hold arbitrary positions.
All inputs are finite; a program needn't handle non-finite values.
Results may differ from a plain program's by a relative error of at most 0.0003.
The roundings to bfloat16 on the way count: a program that leaves them out, or rounds other values in their place, can miss the bound.
Values may be sent and summed in bfloat16 or wider, within the bound.
A program may use at most 64 MiB of HBM per device.

v0:
```python
import jax
import jax.numpy as jnp
from jax import lax
from jax.sharding import PartitionSpec as P


def brick_terms(brick, a_tile, b_tile, c_rows):
    depth, tile, _ = brick.shape
    wide = jnp.dot(
        brick.reshape(depth * tile, tile), b_tile, preferred_element_type=jnp.float32
    ).reshape(depth, tile, -1)
    c_wide = c_rows.astype(jnp.float32)[:, None, :]
    along_a = jnp.sum(wide * c_wide, axis=0)
    deep = jnp.einsum("kij,ir->kjr", brick, a_tile, preferred_element_type=jnp.float32)
    along_b = jnp.sum(deep * c_wide, axis=0)
    along_c = jnp.sum(deep * b_tile.astype(jnp.float32)[None, :, :], axis=1)
    return (along_a, along_b, along_c)


def add_tile(total, delta, start):
    old = lax.dynamic_slice_in_dim(total, start, delta.shape[0], 0)
    return lax.dynamic_update_slice_in_dim(total, old + delta, start, 0)


def gram(values):
    return jnp.dot(values.T, values, preferred_element_type=jnp.float32)


def project(state, hess, drive, rate):
    scale = jnp.sum(jnp.abs(hess), axis=1) + 1e-06
    slope = (
        jnp.dot(state, hess, precision=lax.Precision.HIGHEST, preferred_element_type=jnp.float32)
        - drive
    )
    return jnp.maximum(state - rate * slope / scale[None, :], 0.0)


def shards(bricks, brick_coords, brick_counts, step_sizes, init_a, init_b, init_c):
    slab = bricks[0, 0]
    places = brick_coords[0, 0]
    own = brick_counts[0, 0]
    depth = slab.shape[1]
    tile = slab.shape[2]
    sweeps = step_sizes.shape[0]
    state_a = init_a[0]
    state_b = init_b[0]
    state_c = init_c
    for sweep in range(sweeps):
        a_bf = state_a.astype(jnp.bfloat16)
        b_bf = state_b.astype(jnp.bfloat16)
        c_bf = state_c.astype(jnp.bfloat16)
        a_range = lax.all_gather(a_bf, "col", axis=0, tiled=True)
        b_range = lax.all_gather(b_bf, "row", axis=0, tiled=True)
        local_ga = gram(a_bf)
        local_gb = gram(b_bf)
        gram_a, gram_b = lax.psum((local_ga, local_gb), ("row", "col"))
        gram_c = gram(c_bf)

        def own_step(slot, carry):
            total_a, total_b, total_c = carry
            brick = lax.dynamic_index_in_dim(slab, slot, 0, keepdims=False)
            spot = lax.dynamic_index_in_dim(places, slot, 1, keepdims=False)
            i_low = spot[0] * tile
            j_low = spot[1] * tile
            k_low = spot[2] * depth
            a_tile = lax.dynamic_slice_in_dim(a_range, i_low, tile, 0)
            b_tile = lax.dynamic_slice_in_dim(b_range, j_low, tile, 0)
            c_rows = lax.dynamic_slice_in_dim(c_bf, k_low, depth, 0)
            delta_a, delta_b, delta_c = brick_terms(brick, a_tile, b_tile, c_rows)
            return (
                add_tile(total_a, delta_a, i_low),
                add_tile(total_b, delta_b, j_low),
                add_tile(total_c, delta_c, k_low),
            )

        empty = (
            jnp.zeros(a_range.shape, jnp.float32),
            jnp.zeros(b_range.shape, jnp.float32),
            jnp.zeros(c_bf.shape, jnp.float32),
        )
        drive_a, drive_b, drive_c = lax.fori_loop(0, own, own_step, empty)
        mine_a = lax.psum_scatter(drive_a, "col", scatter_dimension=0, tiled=True)
        mine_b = lax.psum_scatter(drive_b, "row", scatter_dimension=0, tiled=True)
        summed_c = lax.psum(drive_c, ("row", "col"))
        new_c = project(state_c, gram_a * gram_b, summed_c, step_sizes[sweep, 2])
        new_a = project(state_a, gram_b * gram_c, mine_a, step_sizes[sweep, 0])
        new_b = project(state_b, gram_a * gram_c, mine_b, step_sizes[sweep, 1])
        state_a, state_b, state_c = (new_a, new_b, new_c)
    return (state_a[None], state_b[None], state_c)


def solution(mesh):
    placed = (
        P("row", "col", None, None, None, None),
        P("row", "col", None, None),
        P("row", "col"),
        P(),
        P("row", "col", None),
        P("col", "row", None),
        P(),
    )
    return jax.shard_map(
        shards,
        mesh=mesh,
        in_specs=placed,
        out_specs=(P("row", "col", None), P("col", "row", None), P()),
        check_vma=False,
    )
```

profile of v0, /device:TPU:1, one launch (start us, length us, event | category | flops | bytes accessed | tf_op | source)
XLA Modules:
  0.0 371.3 jit_solution(14206926400180580892)
XLA Ops:
  8.1 1.8 fusion.61
  9.9 0.8 bitcast_convert_fusion
  10.7 1.9 fusion.59
  12.6 0.8 bitcast_convert_fusion.1
  13.4 7.3 %all_gather.12 = bf16[256,256]{1,0:T(8,128)(2,1)S(1)} all-gather(bf16[64,256]{1,0:T(8,128)(2,1)S(1)} %bitcast_convert_fusion), channel_id=1, replica_groups=mesh['row'=4,'col'=8] {'row'}, dimensions={0}, use_global_device_ids=true | all-gather | bytes 163840 | tf_op jit(solution)/shard_map/all_gather | solution.py:53
  20.8 17.0 %all_gather.13 = bf16[512,256]{1,0:T(8,128)(2,1)S(1)} all-gather(bf16[64,256]{1,0:T(8,128)(2,1)S(1)} %bitcast_convert_fusion.1), channel_id=1, replica_groups=mesh['row'=4,'col'=8] {'col'}, dimensions={0}, use_global_device_ids=true | all-gather | bytes 294912 | tf_op jit(solution)/shard_map/all_gather | solution.py:52
  38.5 1.0 copy.16
  41.7 138.7 %all-reduce.7.cloned.1.call-done = (f32[256,256]{1,0:T(8,128)}, f32[256,256]{1,0:T(8,128)}, f32[512,256]{0,1:T(8,128)}) async-done(((f32[256,256]{1,0:T(8,128)}, f32[256,256]{1,0:T(8,128)}, f32[512,256]{0,1:T(8,128)}), (f32[256,256]{1,0:T(8,128)}, f32[256,256]{1,0:T(8,128)}, f32[512,256]{0,1:T(8,128)})) %all-reduce.7.cloned.1.call-update) | async-done | bytes 1048592 | tf_op jit(solution)/shard_map/psum | solution.py:56
  180.4 1.5 abs_reduce_fusion.3
  181.9 1.8 fusion.69
  183.9 1.8 fusion.68
  185.7 6.4 %all_gather.14 = bf16[256,256]{1,0:T(8,128)(2,1)S(1)} all-gather(bf16[64,256]{1,0:T(8,128)(2,1)S(1)} %get-tuple-element.215), channel_id=1, replica_groups=mesh['row'=4,'col'=8] {'row'}, dimensions={0}, use_global_device_ids=true | all-gather | bytes 163840 | tf_op jit(solution)/shard_map/all_gather | solution.py:53
  192.1 0.9 fusion.71
  193.0 1.7 fusion.70
  194.8 17.6 %all_gather.15 = bf16[512,256]{1,0:T(8,128)(2,1)S(1)} all-gather(bf16[64,256]{1,0:T(8,128)(2,1)S(1)} %get-tuple-element.219), channel_id=1, replica_groups=mesh['row'=4,'col'=8] {'col'}, dimensions={0}, use_global_device_ids=true | all-gather | bytes 294912 | tf_op jit(solution)/shard_map/all_gather | solution.py:52
  212.3 0.9 fusion.72
  214.1 1.0 copy.23
  215.8 0.7 reduce-scatter.9.cloned.1.call-update
  216.5 138.6 %all-reduce.5.cloned.1.call-done = (f32[256,256]{1,0:T(8,128)}, f32[256,256]{1,0:T(8,128)}, f32[512,256]{0,1:T(8,128)}) async-done(((f32[256,256]{1,0:T(8,128)}, f32[256,256]{1,0:T(8,128)}, f32[512,256]{0,1:T(8,128)}), (f32[256,256]{1,0:T(8,128)}, f32[256,256]{1,0:T(8,128)}, f32[512,256]{0,1:T(8,128)})) %all-reduce.5.cloned.1.call-update) | async-done | bytes 1048592 | tf_op jit(solution)/shard_map/psum | solution.py:56
  355.0 1.5 abs_reduce_fusion
  356.6 1.4 fusion.30
  357.9 1.0 copy.25
  359.0 2.4 fusion.45
  361.3 2.4 fusion.50
  (62 shorter events, 4.4 us)
Async XLA Ops:
  8.0 12.7 %copy-start.4 = (f32[512,256]{1,0:T(8,128)S(1)}, f32[512,256]{1,0:T(8,128)}, u32[]{:S(2)}) copy-start(f32[512,256]{1,0:T(8,128)} %param.17) | copy-start | bytes 1572868
  8.0 172.4 %all-reduce.7.cloned.1.call-start = ((), (), s32[]{:S(2)}) async-start(), calls=%async_computation.9 | async-start | bytes 2097152 | tf_op jit(solution)/shard_map/psum | solution.py:56
  20.7 17.1 %copy-start.16 = (s32[1,1,3,2]{2,3,1,0:T(2,128)S(1)}, s32[1,1,3,2]{2,3,1,0:T(2,128)}, u32[]{:S(2)}) copy-start(s32[1,1,3,2]{2,3,1,0:T(2,128)} %param.12) | copy-start | bytes 76
  38.5 1.1 copy-start.1
  38.5 1.1 copy-start.3
  39.6 1.4 copy-start.12
  39.6 144.3 %reduce-scatter.7.cloned.1.call-start = ((), (), s32[]{:S(2)}) async-start(), calls=%async_computation.5 | async-start | bytes 327680 | tf_op jit(solution)/shard_map/reduce_scatter | solution.py:83
  40.2 152.8 %reduce-scatter.5.cloned.1.call-start = ((), (), s32[]{:S(2)}) async-start(), calls=%async_computation.4 | async-start | bytes 589824 | tf_op jit(solution)/shard_map/reduce_scatter | solution.py:82
  40.8 314.2 %all-reduce.5.cloned.1.call-start = ((), (), s32[]{:S(2)}) async-start(), calls=%async_computation.8 | async-start | bytes 2097152 | tf_op jit(solution)/shard_map/psum | solution.py:56
  180.4 1.5 copy-start.5
  180.4 1.5 copy-start.6
  180.4 1.5 copy-start.11
  181.9 2.0 copy-start.9
  183.7 9.3 %copy-start.10 = (f32[1,64,256]{2,1,0:T(8,128)S(1)}, f32[1,64,256]{2,1,0:T(8,128)}, u32[]{:S(2)}) copy-start(f32[1,64,256]{2,1,0:T(8,128)} %param.15) | copy-start | bytes 196612
  214.0 1.1 copy-start
  214.1 1.1 copy-start.2
  215.1 143.8 %reduce-scatter.11.cloned.1.call-start = ((), (), s32[]{:S(2)}) async-start(), calls=%async_computation.7 | async-start | bytes 327680 | tf_op jit(solution)/shard_map/reduce_scatter | solution.py:83
  215.7 145.6 %reduce-scatter.9.cloned.1.call-start = ((), (), s32[]{:S(2)}) async-start(), calls=%async_computation.6 | async-start | bytes 589824 | tf_op jit(solution)/shard_map/reduce_scatter | solution.py:82
  355.0 1.5 copy-start.7
  355.0 1.5 copy-start.8
  355.0 1.5 copy-start.15
Sparse Core Ops, SparseCore 0:
  39.7 140.6 all-reduce.6
  215.2 139.7 all-reduce.4
Sparse Core Ops, SparseCore 1:
  43.1 34.1 reduce-scatter.6
  79.3 27.9 reduce-scatter.4
  218.6 33.2 reduce-scatter.10
  254.2 27.9 reduce-scatter.8
where the time goes:
time: 373 us; the launch traced here: 371 us
  waiting for transfers between devices  280 us (75%)
  blocking collectives  48.2 us (13%)
  matrix products  20 us (5%)
  between operations  16 us (4%)
  local copies, waits for them, and re-layouts  4.26 us (1%)
    psum x2, waiting for transfers between devices, shards(): gram_a, gram_b = lax.psum((local_ga, local_gb), ('row', 'col'))  277 us
    all_gather x2, blocking collectives, shards(): a_range = lax.all_gather(a_bf, 'col', axis=0, tiled=True)  34.5 us
    all_gather x2, blocking collectives, shards(): b_range = lax.all_gather(b_bf, 'row', axis=0, tiled=True)  13.7 us
    dot_general x6, matrix products, project(): jnp.dot(state, hess, precision=lax.Precision.HIGHEST, preferred_element_t...  11.4 us
    dot_general x6, matrix products, gram(): return jnp.dot(values.T, values, preferred_element_type=jnp.float32)  8.54 us
  transfers between devices with their start and end apart: 6, of which 2 were waited for; matrix products, arithmetic and copies ran while one was open for 4% of the time, Pallas kernels for 0%

commit v1 on v0

v1 whole, which is shorter than its diff:
```python
import functools

import jax
import jax.numpy as jnp
from jax import lax
from jax.experimental import pallas as pl
from jax.experimental.pallas import tpu as pltpu
from jax.sharding import PartitionSpec as P

MESH = pl.DeviceIdType.MESH
F32 = jnp.float32
BF16 = jnp.bfloat16


def gram(values):
    return lax.dot_general(
        values, values, (((0,), (0,)), ((), ())), preferred_element_type=F32
    )


def kernel(
    nr, nc, sems_of,
    places, counts, rates, bricks, meta, init_a, init_b, init_c,
    out_a, out_b, out_c,
    flip, a_all, b_all, c_all, acc_a, acc_b,
    da, da1, da_sum, da2, db, db2,
    cc, cpart, c2, csum, c3,
    sa_part, sa1, sa_full, sb_part, sb1, sb2, sb_full,
    send, recv,
):
    nz = nc // 2
    slots, depth, tile, _ = bricks.shape
    rank = init_a.shape[-1]
    ra, rb = init_a.shape[0], init_b.shape[0]
    sweeps = rates.shape[0]
    k_row = init_c.shape[0] // nr
    k_half = k_row // 2
    spots = k_row // depth
    nzc = c_all.shape[3]
    qa, qb = tile // ra, tile // rb
    tiles_i, tiles_j = nc // qa, nr // qb

    r = lax.axis_index("row")
    c = lax.axis_index("col")
    z = lax.div(c, 2)
    core = lax.rem(c, 2)
    other = 1 - core
    used = [0]
    started = []

    def push(src, dst, row, col):
        at = used[0]
        used[0] += 1
        copy = pltpu.make_async_remote_copy(
            src_ref=src, dst_ref=dst, send_sem=send.at[at], recv_sem=recv.at[at],
            device_id=(row, col), device_id_type=MESH,
        )
        copy.start()
        started.append(copy)
        return copy

    def to_core(src, dst):
        return push(src, dst, r, z * 2 + other)

    def row_peer(step):
        return lax.rem(r + step, nr), lax.rem(r + nr - step, nr)

    def z_peer(step):
        return lax.rem(z + step, nz), lax.rem(z + nz - step, nz)

    barrier = pltpu.get_barrier_semaphore()
    pl.semaphore_signal(barrier, inc=1, device_id=(r, z * 2 + other), device_id_type=MESH)
    for step in range(1, nr):
        pl.semaphore_signal(barrier, inc=1, device_id=(row_peer(step)[0], c), device_id_type=MESH)
    for step in range(1, nz):
        pl.semaphore_signal(
            barrier, inc=1, device_id=(r, z_peer(step)[0] * 2 + core), device_id_type=MESH
        )

    live = [counts[0] > slot for slot in range(slots)]
    spot_i = [jnp.clip(places[0, slot], 0, tiles_i - 1) for slot in range(slots)]
    spot_j = [jnp.clip(places[1, slot], 0, tiles_j - 1) for slot in range(slots)]

    def weights(spot, tiles):
        return [
            [
                jnp.where(jnp.logical_and(live[slot], spot[slot] == at), 1.0, 0.0).astype(F32)
                for at in range(tiles)
            ]
            for slot in range(slots)
        ]

    w_i = weights(spot_i, tiles_i)
    w_j = weights(spot_j, tiles_j)

    state_a = init_a[...]
    state_b = init_b[...]
    state_c = init_c[pl.ds(pl.multiple_of(r * k_row + core * k_half, 8), k_half), :]
    if nzc > 1:
        start_c = r * k_row + core * k_half + z * (k_half // nzc)
        state_c = init_c[pl.ds(pl.multiple_of(start_c, 8), k_half // nzc), :]
    c_all[0] = init_c[...].astype(BF16).reshape(c_all.shape[1:])
    a_all[0, c] = state_a.astype(BF16)
    b_all[0, r] = state_b.astype(BF16)

    pl.semaphore_wait(barrier, 1 + (nr - 1) + (nz - 1))

    def send_b(s):
        return [push(b_all.at[s, r], b_all.at[s, r], row_peer(step)[0], c) for step in range(1, nr)]

    def send_a(s):
        near = to_core(a_all.at[s, c], a_all.at[s, c])
        return near, [
            push(a_all.at[s, c], a_all.at[s, c], r, z_peer(step)[0] * 2 + core)
            for step in range(1, nz)
        ]

    def forward_a(s, far):
        passed = []
        for step in range(1, nz):
            far[step - 1].wait_recv()
            at = z_peer(step)[1] * 2 + core
            passed.append(to_core(a_all.at[s, at], a_all.at[s, at]))
        return passed

    def forward_row(ref_at, far):
        passed = [to_core(ref_at(r), ref_at(r))]
        for step in range(1, nr):
            far[step - 1].wait_recv()
            at = row_peer(step)[1]
            passed.append(to_core(ref_at(at), ref_at(at)))
        return passed

    def spread_row(ref_at):
        return [push(ref_at(r), ref_at(r), row_peer(step)[0], c) for step in range(1, nr)]

    def spread_c(ref_at):
        if nzc == 1:
            return []
        return [
            push(ref_at(z), ref_at(z), r, z_peer(step)[0] * 2 + core) for step in range(1, nz)
        ]

    def done(copies):
        for copy in copies:
            copy.wait_recv()

    def total(ref, s, count):
        value = ref[s, 0]
        for at in range(1, count):
            value = value + ref[s, at]
        return value

    far_b = send_b(0)
    near_a, far_a = send_a(0)
    for slot in range(slots):
        def turn(k, carry, slot=slot):
            flip[slot, k] = bricks[slot, k].T
            return carry
        lax.fori_loop(0, depth, turn, 0)
    gram_c = gram(c_all[0].reshape(nr * k_row, rank))
    wait_c = None

    for s in range(sweeps):
        done(far_b)
        sb_part[s] = gram(b_all[s].reshape(nr * rb, rank)).reshape(sb_part.shape[1:])
        step_sb1 = to_core(sb_part.at[s, r, other], sb1.at[s])
        passed_a = forward_a(s, far_a)
        step_sb1.wait_recv()
        sb2[s, z] = sb_part[s, r, core] + sb1[s]
        step_sb2 = [
            push(sb2.at[s, z], sb2.at[s, z], r, z_peer(step)[0] * 2 + core)
            for step in range(1, nz)
        ]
        near_a.wait_recv()
        done(passed_a)
        sa_part[s] = gram(a_all[s].reshape(nc * ra, rank)).reshape(sa_part.shape[1:])
        sa1[s, r] = sa_part[s, core, r]
        step_sa1 = [
            push(sa_part.at[s, core, row_peer(step)[0]], sa1.at[s, r], row_peer(step)[0], c)
            for step in range(1, nr)
        ]
        if wait_c is not None:
            wait_c()

        def tile_b(slot):
            return b_all[s, pl.ds(spot_j[slot] * qb, qb)].reshape(tile, rank)

        def rows_c(slot):
            at = jnp.clip(places[2, slot], 0, nr * spots - 1)
            within = lax.rem(at, spots)
            low = lax.rem(within, spots // 2)
            wide_c = c_all[s, lax.div(at, spots), lax.div(within, spots // 2)]
            picked = jnp.zeros((depth, rank), F32)
            flat = wide_c.astype(F32).reshape(spots // 2, depth, rank)
            for one in range(spots // 2):
                picked = picked + flat[one] * jnp.where(low == one, 1.0, 0.0).astype(F32)
            return picked

        c_rows = [rows_c(slot) for slot in range(slots)]
        for slot in range(slots):
            b_tile = tile_b(slot)
            sums = jnp.zeros((tile, rank), F32)
            for k in range(depth):
                wide = jnp.dot(bricks[slot, k], b_tile, preferred_element_type=F32)
                sums = sums + wide * c_rows[slot][k:k + 1]
            acc_a[slot] = sums
        for g in range(nc):
            at, off = g // qa, (g % qa) * ra
            da[s, g % 2, g // 2] = sum(
                w_i[slot][at] * acc_a[slot, off:off + ra, :] for slot in range(slots)
            )
        step_da1 = {}
        for step in list(range(1, nz)) + [0]:
            to = z_peer(step)[0]
            step_da1[step] = to_core(da.at[s, other, to], da1.at[s, to])

        done(step_sa1)
        sa_full[s, core, r] = total(sa1, s, nr)
        step_sa2 = spread_row(lambda at: sa_full.at[s, core, at])

        for slot in range(slots):
            a_tile = a_all[s, pl.ds(spot_i[slot] * qa, qa)].reshape(tile, rank)
            b_tile = tile_b(slot).astype(F32)
            sums = jnp.zeros((tile, rank), F32)
            along_c = []
            for k in range(depth):
                deep = jnp.dot(flip[slot, k], a_tile, preferred_element_type=F32)
                sums = sums + deep * c_rows[slot][k:k + 1]
                along_c.append(jnp.sum(deep * b_tile, axis=0, keepdims=True))
            acc_b[slot] = sums
            cc[s, r, slot * depth:(slot + 1) * depth, :] = jnp.concatenate(along_c, axis=0)
        cc[s, r, slots * depth:, :] = meta[...]
        step_c1 = spread_row(lambda at: cc.at[s, at])
        for g in range(nr):
            at, off = g // qb, (g % qb) * rb
            db[s, g] = sum(
                w_j[slot][at] * acc_b[slot, off:off + rb, :] for slot in range(slots)
            )
        db2[s, r] = db[s, r]
        step_db = [
            push(db.at[s, row_peer(step)[0]], db2.at[s, r], row_peer(step)[0], c)
            for step in range(1, nr)
        ]

        step_da2 = []
        for step in list(range(1, nz)) + [0]:
            to = z_peer(step)[0]
            step_da1[step].wait_recv()
            if step == 0:
                da2[s, z] = da[s, core, z] + da1[s, z]
            else:
                da_sum[s, to] = da[s, core, to] + da1[s, to]
                step_da2.append(push(da_sum.at[s, to], da2.at[s, z], r, to * 2 + core))

        done(step_sb2)
        sb_full[s, r, core] = total(sb2, s, nz)
        step_sb3 = spread_row(lambda at: sb_full.at[s, at, core])
        step_sa3 = forward_row(lambda at: sa_full.at[s, core, at], step_sa2)

        done(step_c1)
        for one in range(spots):
            want = (r * spots + one).astype(F32)
            sums = jnp.zeros((depth, rank), F32)
            for src in range(nr):
                for slot in range(slots):
                    tag = cc[s, src, slots * depth + slot:slots * depth + slot + 1, :]
                    term = cc[s, src, slot * depth:(slot + 1) * depth, :]
                    sums = sums + jnp.where(tag == want, term, 0.0)
            half = spots // 2
            cpart[s, one // half, (one % half) * depth:(one % half + 1) * depth, :] = sums
        step_c2 = to_core(cpart.at[s, other], c2.at[s])
        step_sb4 = forward_row(lambda at: sb_full.at[s, at, core], step_sb3)
        step_c2.wait_recv()
        csum[s] = (cpart[s, core] + c2[s]).reshape(csum.shape[1:])
        mine = z if nzc > 1 else 0
        c3[s, z] = csum[s, mine]
        step_c3 = []
        for step in range(1, nz):
            to = z_peer(step)[0]
            step_c3.append(
                push(csum.at[s, to if nzc > 1 else 0], c3.at[s, z], r, to * 2 + core)
            )

        def prepare(state, hess):
            scale = jnp.sum(jnp.abs(hess), axis=0, keepdims=True) + 1e-06
            moved = jnp.dot(
                state, hess, precision=lax.Precision.HIGHEST, preferred_element_type=F32
            )
            return moved, scale

        def finish(state, ready, drive, rate):
            moved, scale = ready
            return jnp.maximum(state - rate * (moved - drive) / scale, 0.0)

        last = s == sweeps - 1
        done(step_sa3)
        gram_a = sa_full[s].reshape(rank, rank)
        ready_b = prepare(state_b, gram_a * gram_c)
        done(step_db)
        state_b = finish(state_b, ready_b, total(db2, s, nr), rates[s, 1])
        if last:
            out_b[...] = state_b
        else:
            b_all[s + 1, r] = state_b.astype(BF16)
            far_b = send_b(s + 1)
        done(step_sb4)
        gram_b = sb_full[s].reshape(rank, rank)
        ready_c = prepare(state_c, gram_a * gram_b)
        done(step_c3)
        state_c = finish(state_c, ready_c, total(c3, s, nz), rates[s, 2])
        if last:
            part = lambda at: out_c.at[r, core, at]
            rows = lambda at: out_c.at[at, core]
            out_c[r, core, mine] = state_c
        else:
            part = lambda at, s=s: c_all.at[s + 1, r, core, at]
            rows = lambda at, s=s: c_all.at[s + 1, at, core]
            c_all[s + 1, r, core, mine] = state_c.astype(BF16)
        far_c = spread_c(part)
        ready_a = prepare(state_a, gram_b * gram_c)
        done(step_da2)
        state_a = finish(state_a, ready_a, total(da2, s, nz), rates[s, 0])
        if last:
            out_a[...] = state_a
        else:
            a_all[s + 1, c] = state_a.astype(BF16)
            near_a, far_a = send_a(s + 1)
        done(far_c)
        far_c = spread_row(rows)
        if last:
            done(forward_row(rows, far_c))
        else:
            passed_c = forward_row(rows, far_c)
            done(passed_c)
            gram_c = gram(c_all[s + 1].reshape(nr * k_row, rank))

    for copy in started:
        copy.wait_send()
    assert used[0] <= sems_of


def shards(nr, nc, bricks, brick_coords, brick_counts, step_sizes, init_a, init_b, init_c):
    slab = bricks[0, 0]
    places = brick_coords[0, 0]
    counts = brick_counts[0]
    slots, depth, tile, _ = slab.shape
    sweeps = step_sizes.shape[0]
    ra, rank = init_a.shape[1:]
    rb = init_b.shape[1]
    depth_c = init_c.shape[0]
    nz = nc // 2
    k_row = depth_c // nr
    k_half = k_row // 2
    nzc = nz if k_half % (nz * 16) == 0 else 1
    rc = k_half // nzc
    tags = -(-slots // 8) * 8
    alive = jnp.arange(slots) < counts[0]
    tag = jnp.where(alive, places[2], -1).astype(F32)
    meta = jnp.broadcast_to(jnp.pad(tag, (0, tags - slots))[:, None], (tags, rank))
    sems = sweeps * (2 * nz + 1 + (nr - 1) + 2 + nz + 4 * nr + nz + nz + 2 * nr + nr + 1 + nz + nz + 6 * nr)
    vmem = pl.BlockSpec(memory_space=pltpu.VMEM)
    smem = pl.BlockSpec(memory_space=pltpu.SMEM)
    scratch = [
        ((slots, depth, tile, tile), BF16),
        ((sweeps, nc, ra, rank), BF16),
        ((sweeps, nr, rb, rank), BF16),
        ((sweeps, nr, 2, nzc, rc, rank), BF16),
        ((slots, tile, rank), F32),
        ((slots, tile, rank), F32),
        ((sweeps, 2, nz, ra, rank), F32),
        ((sweeps, nz, ra, rank), F32),
        ((sweeps, nz, ra, rank), F32),
        ((sweeps, nz, ra, rank), F32),
        ((sweeps, nr, rb, rank), F32),
        ((sweeps, nr, rb, rank), F32),
        ((sweeps, nr, slots * depth + tags, rank), F32),
        ((sweeps, 2, k_half, rank), F32),
        ((sweeps, k_half, rank), F32),
        ((sweeps, nzc, rc, rank), F32),
        ((sweeps, nz, rc, rank), F32),
        ((sweeps, 2, nr, rank // nr // 2, rank), F32),
        ((sweeps, nr, rank // nr // 2, rank), F32),
        ((sweeps, 2, nr, rank // nr // 2, rank), F32),
        ((sweeps, nr, 2, rank // nr // 2, rank), F32),
        ((sweeps, rank // nr // 2, rank), F32),
        ((sweeps, nz, rank // nr // 2, rank), F32),
        ((sweeps, nr, 2, rank // nr // 2, rank), F32),
    ]
    new_a, new_b, new_c = pl.pallas_call(
        functools.partial(kernel, nr, nc, sems),
        out_shape=(
            jax.ShapeDtypeStruct((ra, rank), F32),
            jax.ShapeDtypeStruct((rb, rank), F32),
            jax.ShapeDtypeStruct((nr, 2, nzc, rc, rank), F32),
        ),
        in_specs=[smem, smem, smem] + [vmem] * 5,
        out_specs=(vmem, vmem, vmem),
        scratch_shapes=[pltpu.VMEM(*one) for one in scratch]
        + [pltpu.SemaphoreType.DMA((sems,)), pltpu.SemaphoreType.DMA((sems,))],
        compiler_params=pltpu.CompilerParams(
            collective_id=0, has_side_effects=True, vmem_limit_bytes=48 * 1024 * 1024
        ),
        name="sweeps",
    )(places, counts, step_sizes, slab, meta, init_a[0], init_b[0], init_c)
    return new_a[None], new_b[None], new_c.reshape(depth_c, rank)


def solution(mesh):
    placed = (
        P("row", "col", None, None, None, None),
        P("row", "col", None, None),
        P("row", "col"),
        P(),
        P("row", "col", None),
        P("col", "row", None),
        P(),
    )
    return jax.shard_map(
        functools.partial(shards, mesh.shape["row"], mesh.shape["col"]),
        mesh=mesh,
        in_specs=placed,
        out_specs=(P("row", "col", None), P("col", "row", None), P()),
        check_vma=False,
    )
```

time: 373 us -> 75.7 us (0.20)
  waiting for transfers between devices: 280 us -> 0 us
  Pallas kernels: 0 us -> 66.5 us
  blocking collectives: 48.2 us -> 0 us
  matrix products: 20 us -> 0 us
  between operations: 16 us -> 1.3 us
    psum x2 -> x0, waiting for transfers between devices: 277 us -> none  [shards(): gram_a, gram_b = lax.psum((local_ga, local_gb), ('row', 'col'))]
    pallas_call x0 -> x1, Pallas kernels: none -> 66.5 us  [shards(): pl.pallas_call(functools.partial(kernel, nr, nc, sems), out_shape=(jax.Sh...]
    all_gather x4 -> x0, blocking collectives: 48.2 us -> none  [the longest x2 34.5 us: shards(): a_range = lax.all_gather(a_bf, 'col', axis=0, tiled=True)]
    dot_general x12 -> x0, matrix products: 20 us -> none  [the longest x6 11.4 us: project(): jnp.dot(state, hess, precision=lax.Precision.HIGHEST, preferred_element_t...]
    unnamed x32 -> x15, local copies, waits for them, and re-layouts: 1.26 us -> 7.28 us
  transfers between devices with their start and end apart: 6 -> 0, of which waited for: 2 -> 0; matrix products, arithmetic and copies ran while one was open for 4% -> 0% of each run, Pallas kernels for 0% -> 0%
where the time goes in v1:
time: 75.7 us; the launch traced here: 75.4 us
  Pallas kernels  66.5 us (88%)
  local copies, waits for them, and re-layouts  7.63 us (10%)
  between operations  1.3 us (2%)
    pallas_call x1, Pallas kernels, shards(): pl.pallas_call(functools.partial(kernel, nr, nc, sems), out_shape=(jax.Sh...  66.5 us
    unnamed x15, local copies, waits for them, and re-layouts  7.28 us

profile of v1, /device:TPU:1, one launch (start us, length us, event | category | flops | bytes accessed | tf_op | source)
XLA Modules:
  0.0 75.4 jit_solution(11741701971872869356)
XLA Ops:
  1.3 0.0 copy-start.5
  1.3 0.7 copy-done.5
  2.0 0.2 slice_reduce_fusion
  2.2 0.1 copy.10.places
  2.3 0.0 copy-start.4
  2.3 0.1 broadcast_in_dim.17.meta
  2.3 0.6 copy-done.4
  2.9 0.0 copy-start
  2.9 1.2 %copy-done = bf16[1,1,2,16,128,128]{5,4,3,2,1,0:T(8,128)(2,1)S(1)} copy-done((bf16[1,1,2,16,128,128]{5,4,3,2,1,0:T(8,128)(2,1)S(1)}, bf16[1,1,2,16,128,128]{5,4,3,2,1,0:T(8,128)(2,1)}, u32[]{:S(2)}) %copy-start) | copy-done | bytes 1048600
  4.2 0.0 copy-start.1
  4.2 1.0 %copy-done.1 = f32[512,256]{1,0:T(8,128)S(1)} copy-done((f32[512,256]{1,0:T(8,128)S(1)}, f32[512,256]{1,0:T(8,128)}, u32[]{:S(2)}) %copy-start.1) | copy-done | bytes 524312
  5.2 0.0 copy-start.2
  5.2 0.8 %copy-done.2 = f32[1,64,256]{2,1,0:T(8,128)S(1)} copy-done((f32[1,64,256]{2,1,0:T(8,128)S(1)}, f32[1,64,256]{2,1,0:T(8,128)}, u32[]{:S(2)}) %copy-start.2) | copy-done | bytes 65560
  6.0 0.0 copy-start.3
  6.0 0.8 %copy-done.3 = f32[1,64,256]{2,1,0:T(8,128)S(1)} copy-done((f32[1,64,256]{2,1,0:T(8,128)S(1)}, f32[1,64,256]{2,1,0:T(8,128)}, u32[]{:S(2)}) %copy-start.3) | copy-done | bytes 65560
  6.9 66.5 %sweeps.1 = (f32[64,256]{1,0:T(8,128)S(1)}, f32[64,256]{1,0:T(8,128)S(1)}, f32[4,2,4,16,256]{4,3,2,1,0:T(8,128)S(1)}) custom-call(s32[3,2]{1,0:T(4,128)S(1)} %copy.10.places, s32[1]{0:T(128)} %bitcast.9.counts, f32[2,3]{1,0:T(2,128)S(1)} %copy-done.4, bf16[2,16,128,128]{3,2,1,0:T(8,128)(2,1)S(1)} %bitcast.11, f32[8,256]{1,0:T(8,128)S(1)} %broadcast_in_dim.17.meta, ...), custom_call_target="tpu_custom_call" | custom-call | tf_op jit(solution)/shard_map/sweeps/pallas_call | solution.py:390
  73.3 0.6 copy.15
  74.0 0.6 copy.16
  74.6 0.8 %copy.17 = f32[512,256]{1,0:T(8,128)} copy(f32[512,256]{1,0:T(8,128)S(1)} %bitcast.12) | data formatting | bytes 1048576
  (2 shorter events, 0.0 us)
Async XLA Ops:
  1.3 0.7 copy-start.5
  2.3 0.7 copy-start.4
  2.9 1.2 %copy-start = (bf16[1,1,2,16,128,128]{5,4,3,2,1,0:T(8,128)(2,1)S(1)}, bf16[1,1,2,16,128,128]{5,4,3,2,1,0:T(8,128)(2,1)}, u32[]{:S(2)}) copy-start(bf16[1,1,2,16,128,128]{5,4,3,2,1,0:T(8,128)(2,1)} %param.7) | copy-start | bytes 3145732
  4.2 1.0 %copy-start.1 = (f32[512,256]{1,0:T(8,128)S(1)}, f32[512,256]{1,0:T(8,128)}, u32[]{:S(2)}) copy-start(f32[512,256]{1,0:T(8,128)} %init_c.1) | copy-start | bytes 1572868
  5.2 0.8 %copy-start.2 = (f32[1,64,256]{2,1,0:T(8,128)S(1)}, f32[1,64,256]{2,1,0:T(8,128)}, u32[]{:S(2)}) copy-start(f32[1,64,256]{2,1,0:T(8,128)} %param.11) | copy-start | bytes 196612
  6.0 0.8 %copy-start.3 = (f32[1,64,256]{2,1,0:T(8,128)S(1)}, f32[1,64,256]{2,1,0:T(8,128)}, u32[]{:S(2)}) copy-start(f32[1,64,256]{2,1,0:T(8,128)} %param.12) | copy-start | bytes 196612

commit v2 on v1

v2 whole, which is shorter than its diff:
```python
import functools

import jax
import jax.numpy as jnp
from jax import lax
from jax.experimental import pallas as pl
from jax.experimental.pallas import tpu as pltpu
from jax.sharding import PartitionSpec as P

MESH = pl.DeviceIdType.MESH
F32 = jnp.float32
BF16 = jnp.bfloat16


def gram(values):
    return lax.dot_general(
        values, values, (((0,), (0,)), ((), ())), preferred_element_type=F32
    )


def kernel(
    nr, nc, sems_of,
    places, counts, rates, far_bricks, far_a0, far_b0, far_c0,
    out_a, out_b, out_c,
    bricks, init_a, init_b, init_c,
    flip, a_all, b_all, c_all, acc_a, acc_b, spread,
    da, da1, da_sum, da2, db, db2,
    cc, tags, csum, c3,
    sa_part, sa1, sa_full, sb_part, sb1, sb2, sb_full,
    load, send, recv,
):
    nz = nc // 2
    slots, depth, tile, _ = bricks.shape
    rank = init_a.shape[-1]
    ra, rb = init_a.shape[0], init_b.shape[0]
    sweeps = rates.shape[0]
    k_row = init_c.shape[0] // nr
    k_half = k_row // 2
    spots = k_row // depth
    nzc = c_all[0].shape[2]
    qa, qb = tile // ra, tile // rb
    tiles_i, tiles_j = nc // qa, nr // qb

    loads = [
        pltpu.make_async_copy(src, dst, load.at[at])
        for at, (src, dst) in enumerate(
            ((far_b0, init_b), (far_a0, init_a), (far_c0, init_c), (far_bricks, bricks))
        )
    ]
    for copy in loads:
        copy.start()

    r = lax.axis_index("row")
    c = lax.axis_index("col")
    z = lax.div(c, 2)
    core = lax.rem(c, 2)
    other = 1 - core
    used = [0]
    started = []

    def push(src, dst, row, col):
        at = used[0]
        used[0] += 1
        copy = pltpu.make_async_remote_copy(
            src_ref=src, dst_ref=dst, send_sem=send.at[at], recv_sem=recv.at[at],
            device_id=(row, col), device_id_type=MESH,
        )
        copy.start()
        started.append(copy)
        return copy

    def to_core(src, dst):
        return push(src, dst, r, z * 2 + other)

    def row_peer(step):
        return lax.rem(r + step, nr), lax.rem(r + nr - step, nr)

    def z_peer(step):
        return lax.rem(z + step, nz), lax.rem(z + nz - step, nz)

    barrier = pltpu.get_barrier_semaphore()
    pl.semaphore_signal(barrier, inc=1, device_id=(r, z * 2 + other), device_id_type=MESH)
    for step in range(1, nr):
        for col in (c, z * 2 + other):
            pl.semaphore_signal(
                barrier, inc=1, device_id=(row_peer(step)[0], col), device_id_type=MESH
            )
    for step in range(1, nz):
        pl.semaphore_signal(
            barrier, inc=1, device_id=(r, z_peer(step)[0] * 2 + core), device_id_type=MESH
        )

    live = [counts[0, 0] > slot for slot in range(slots)]
    spot_i = [jnp.clip(places[0, 0, slot, 0], 0, tiles_i - 1) for slot in range(slots)]
    spot_j = [jnp.clip(places[0, 0, slot, 1], 0, tiles_j - 1) for slot in range(slots)]

    def weights(spot, tiles):
        return [
            [
                jnp.where(jnp.logical_and(live[slot], spot[slot] == at), 1.0, 0.0).astype(F32)
                for at in range(tiles)
            ]
            for slot in range(slots)
        ]

    w_i = weights(spot_i, tiles_i)
    w_j = weights(spot_j, tiles_j)

    spot_k = [jnp.clip(places[0, 0, slot, 2], 0, nr * spots - 1) for slot in range(slots)]
    number = lax.broadcasted_iota(jnp.int32, tags.shape[2:], 0)
    tag = jnp.full(tags.shape[2:], -1.0, F32)
    for slot in range(slots):
        mark = jnp.where(live[slot], spot_k[slot], -1).astype(F32)
        tag = jnp.where(number == slot, mark, tag)
    tags[r, core] = tag

    loads[0].wait()
    state_b = init_b[...]
    b_all[0][r] = state_b.astype(BF16)
    loads[1].wait()
    state_a = init_a[...]
    a_all[0][c] = state_a.astype(BF16)

    pl.semaphore_wait(barrier, 1 + 2 * (nr - 1) + (nz - 1))

    def send_b(s):
        return [push(b_all[s].at[r], b_all[s].at[r], row_peer(step)[0], c) for step in range(1, nr)]

    def send_a(s):
        near = to_core(a_all[s].at[c], a_all[s].at[c])
        return near, [
            push(a_all[s].at[c], a_all[s].at[c], r, z_peer(step)[0] * 2 + core)
            for step in range(1, nz)
        ]

    def forward_a(s, far):
        passed = []
        for step in range(1, nz):
            far[step - 1].wait_recv()
            at = z_peer(step)[1] * 2 + core
            passed.append(to_core(a_all[s].at[at], a_all[s].at[at]))
        return passed

    def forward_row(ref_at, far):
        passed = [to_core(ref_at(r), ref_at(r))]
        for step in range(1, nr):
            far[step - 1].wait_recv()
            at = row_peer(step)[1]
            passed.append(to_core(ref_at(at), ref_at(at)))
        return passed

    def spread_row(ref_at):
        return [push(ref_at(r), ref_at(r), row_peer(step)[0], c) for step in range(1, nr)]

    def spread_chips(ref):
        copies = [to_core(ref, ref)]
        for step in range(1, nr):
            for col in (c, z * 2 + other):
                copies.append(push(ref, ref, row_peer(step)[0], col))
        return copies

    def spread_c(ref_at):
        if nzc == 1:
            return []
        return [
            push(ref_at(z), ref_at(z), r, z_peer(step)[0] * 2 + core) for step in range(1, nz)
        ]

    def done(copies):
        for copy in copies:
            copy.wait_recv()

    def total(ref, s, count):
        value = ref[s, 0]
        for at in range(1, count):
            value = value + ref[s, at]
        return value

    def turn(slot):
        def one(k, carry):
            flip[slot, k] = bricks[slot, k].T
            return carry
        lax.fori_loop(0, depth, one, 0, unroll=4)

    def tile_a(s, slot):
        return a_all[s][pl.ds(spot_i[slot] * qa, qa)].reshape(tile, rank)

    def tile_b(s, slot):
        return b_all[s][pl.ds(spot_j[slot] * qb, qb)].reshape(tile, rank)

    def rows_c(s, slot):
        at = spot_k[slot]
        within = lax.rem(at, spots)
        low = lax.rem(within, spots // 2)
        wide_c = c_all[s][lax.div(at, spots), lax.div(within, spots // 2)]
        flat = wide_c.astype(F32).reshape(spots // 2, depth, rank)
        picked = jnp.zeros((depth, rank), F32)
        for one in range(spots // 2):
            picked = picked + flat[one] * jnp.where(low == one, 1.0, 0.0).astype(F32)
        return picked

    strip = 8
    batch = 4

    def fill(value_at, right):
        for k in range(0, depth, batch):
            spread[k * tile:(k + batch) * tile, :] = jnp.dot(
                value_at(k).reshape(batch * tile, tile), right, preferred_element_type=F32
            )

    def wide_pass(s, slot):
        fill(lambda k: bricks[slot, k:k + batch], tile_b(s, slot))
        c_rows = rows_c(s, slot)
        acc_b[slot] = tile_a(s, slot).astype(F32)

        def body(at, carry):
            low = pl.multiple_of(at * strip, strip)
            a_rows = acc_b[slot, pl.ds(low, strip), :]
            sums = jnp.zeros((strip, rank), F32)
            along_c = []
            for k in range(depth):
                part = spread[pl.ds(pl.multiple_of(k * tile + low, strip), strip), :]
                sums = sums + part * c_rows[k:k + 1]
                along_c.append(carry[k] + part * a_rows)
            acc_a[slot, pl.ds(low, strip), :] = sums
            return tuple(along_c)

        empty = tuple(jnp.zeros((strip, rank), F32) for _ in range(depth))
        along_c = lax.fori_loop(0, tile // strip, body, empty)
        cc[s, r, core, slot * depth:(slot + 1) * depth, :] = jnp.concatenate(
            [jnp.sum(one, axis=0, keepdims=True) for one in along_c], axis=0
        )

    def deep_pass(s, slot):
        fill(lambda k: flip[slot, k:k + batch], tile_a(s, slot))
        c_rows = rows_c(s, slot)

        def body(at, carry):
            low = pl.multiple_of(at * strip, strip)
            sums = jnp.zeros((strip, rank), F32)
            for k in range(depth):
                part = spread[pl.ds(pl.multiple_of(k * tile + low, strip), strip), :]
                sums = sums + part * c_rows[k:k + 1]
            acc_b[slot, pl.ds(low, strip), :] = sums
            return carry

        lax.fori_loop(0, tile // strip, body, 0)

    far_b = send_b(0)
    near_a, far_a = send_a(0)
    far_tags = spread_chips(tags.at[r, core])
    loads[2].wait()
    mine = z if nzc > 1 else 0
    start_c = r * k_row + core * k_half + mine * (k_half // nzc)
    state_c = init_c[pl.ds(pl.multiple_of(start_c, 8), k_half // nzc), :]
    c_all[0][...] = init_c[...].astype(BF16).reshape(c_all[0].shape)
    gram_c = gram(c_all[0][...].reshape(nr * k_row, rank))
    loads[3].wait()
    wait_c = []

    for s in range(sweeps):
        done(far_b)
        sb_part[s] = gram(b_all[s][...].reshape(nr * rb, rank)).reshape(sb_part.shape[1:])
        step_sb1 = to_core(sb_part.at[s, r, other], sb1.at[s])
        passed_a = forward_a(s, far_a)
        step_sb1.wait_recv()
        sb2[s, z] = sb_part[s, r, core] + sb1[s]
        step_sb2 = [
            push(sb2.at[s, z], sb2.at[s, z], r, z_peer(step)[0] * 2 + core)
            for step in range(1, nz)
        ]
        near_a.wait_recv()
        done(passed_a)
        sa_part[s] = gram(a_all[s][...].reshape(nc * ra, rank)).reshape(sa_part.shape[1:])
        sa1[s, r] = sa_part[s, core, r]
        step_sa1 = [
            push(sa_part.at[s, core, row_peer(step)[0]], sa1.at[s, r], row_peer(step)[0], c)
            for step in range(1, nr)
        ]
        done(wait_c)
        for slot in range(slots):
            wide_pass(s, slot)
        step_c1 = spread_chips(cc.at[s, r, core])
        for g in range(nc):
            at, off = g // qa, (g % qa) * ra
            da[s, g % 2, g // 2] = sum(
                w_i[slot][at] * acc_a[slot, off:off + ra, :] for slot in range(slots)
            )
        step_da1 = {}
        for step in list(range(1, nz)) + [0]:
            to = z_peer(step)[0]
            step_da1[step] = to_core(da.at[s, other, to], da1.at[s, to])

        done(step_sa1)
        sa_full[s, core, r] = total(sa1, s, nr)
        step_sa2 = spread_row(lambda at: sa_full.at[s, core, at])
        done(step_sb2)
        sb_full[s, r, core] = total(sb2, s, nz)
        step_sb3 = spread_row(lambda at: sb_full.at[s, at, core])

        step_da2 = []
        for step in list(range(1, nz)) + [0]:
            to = z_peer(step)[0]
            step_da1[step].wait_recv()
            if step == 0:
                da2[s, z] = da[s, core, z] + da1[s, z]
            else:
                da_sum[s, to] = da[s, core, to] + da1[s, to]
                step_da2.append(push(da_sum.at[s, to], da2.at[s, z], r, to * 2 + core))

        done(step_c1)
        if s == 0:
            done(far_tags)
        half = spots // 2
        found = []
        for one in range(half):
            want = (r * spots + core * half + one).astype(F32)
            sums = jnp.zeros((depth, rank), F32)
            for src in range(nr):
                for side in range(2):
                    for slot in range(slots):
                        term = cc[s, src, side, slot * depth:(slot + 1) * depth, :]
                        mark = tags[src, side, slot:slot + 1, :]
                        sums = sums + jnp.where(mark == want, term, 0.0)
            found.append(sums)
        csum[s] = jnp.concatenate(found, axis=0).reshape(csum.shape[1:])
        c3[s, z] = csum[s, mine]
        step_c3 = []
        for step in range(1, nz):
            to = z_peer(step)[0]
            step_c3.append(
                push(csum.at[s, to if nzc > 1 else 0], c3.at[s, z], r, to * 2 + core)
            )

        for slot in range(slots):
            if s == 0:
                turn(slot)
            deep_pass(s, slot)
        for g in range(nr):
            at, off = g // qb, (g % qb) * rb
            db[s, g] = sum(
                w_j[slot][at] * acc_b[slot, off:off + rb, :] for slot in range(slots)
            )
        db2[s, r] = db[s, r]
        step_db = [
            push(db.at[s, row_peer(step)[0]], db2.at[s, r], row_peer(step)[0], c)
            for step in range(1, nr)
        ]

        step_sa3 = forward_row(lambda at: sa_full.at[s, core, at], step_sa2)
        step_sb4 = forward_row(lambda at: sb_full.at[s, at, core], step_sb3)

        def prepare(state, hess):
            scale = jnp.sum(jnp.abs(hess), axis=0, keepdims=True) + 1e-06
            high = hess.astype(BF16)
            low = (hess - high.astype(F32)).astype(BF16)
            top = state.astype(BF16)
            rest = (state - top.astype(F32)).astype(BF16)
            rows = state.shape[0]
            both = jnp.dot(
                jnp.concatenate([top, rest], axis=0), high, preferred_element_type=F32
            )
            moved = both[:rows] + both[rows:] + jnp.dot(top, low, preferred_element_type=F32)
            return moved, scale

        def finish(state, ready, drive, rate):
            moved, scale = ready
            return jnp.maximum(state - rate * (moved - drive) / scale, 0.0)

        last = s == sweeps - 1
        done(step_sa3)
        gram_a = sa_full[s].reshape(rank, rank)
        done(step_sb4)
        gram_b = sb_full[s].reshape(rank, rank)
        ready_c = prepare(state_c, gram_a * gram_b)
        done(step_c3)
        state_c = finish(state_c, ready_c, total(c3, s, nz), rates[s, 2])
        if last:
            out_c[r, core, mine] = state_c
            far_c = spread_c(lambda at: out_c.at[r, core, at])
        else:
            c_all[s + 1][r, core, mine] = state_c.astype(BF16)
            far_c = spread_c(lambda at: c_all[s + 1].at[r, core, at])
        ready_b = prepare(state_b, gram_a * gram_c)
        done(step_db)
        state_b = finish(state_b, ready_b, total(db2, s, nr), rates[s, 1])
        if last:
            out_b[...] = state_b
        else:
            b_all[s + 1][r] = state_b.astype(BF16)
            far_b = send_b(s + 1)
        done(far_c)
        if last:
            far_c = spread_row(lambda at: out_c.at[at, core])
        else:
            wait_c = spread_chips(c_all[s + 1].at[r, core])
        ready_a = prepare(state_a, gram_b * gram_c)
        done(step_da2)
        state_a = finish(state_a, ready_a, total(da2, s, nz), rates[s, 0])
        if last:
            out_a[...] = state_a
            done(forward_row(lambda at: out_c.at[at, core], far_c))
        else:
            a_all[s + 1][c] = state_a.astype(BF16)
            near_a, far_a = send_a(s + 1)
            done(wait_c)
            wait_c = []
            gram_c = gram(c_all[s + 1][...].reshape(nr * k_row, rank))

    for copy in started:
        copy.wait_send()
    assert used[0] <= sems_of


def shards(nr, nc, bricks, brick_coords, brick_counts, step_sizes, init_a, init_b, init_c):
    slots, depth, tile, _ = bricks.shape[2:]
    sweeps = step_sizes.shape[0]
    ra, rank = init_a.shape[1:]
    rb = init_b.shape[1]
    depth_c = init_c.shape[0]
    nz = nc // 2
    k_row = depth_c // nr
    k_half = k_row // 2
    nzc = nz if k_half % (nz * 16) == 0 else 1
    rc = k_half // nzc
    tags = -(-slots // 8) * 8
    sems = 2 * nr + sweeps * (6 * nz + 13 * nr)
    vmem = pl.BlockSpec(memory_space=pltpu.VMEM)
    smem = pl.BlockSpec(memory_space=pltpu.SMEM)
    far = pl.BlockSpec(memory_space=pltpu.HBM)
    scratch = [
        ((slots, depth, tile, tile), BF16),
        ((ra, rank), F32),
        ((rb, rank), F32),
        ((depth_c, rank), F32),
        ((slots, depth, tile, tile), BF16),
        [((nc, ra, rank), BF16)] * sweeps,
        [((nr, rb, rank), BF16)] * sweeps,
        [((nr, 2, nzc, rc, rank), BF16)] * sweeps,
        ((slots, tile, rank), F32),
        ((slots, tile, rank), F32),
        ((depth * tile, rank), F32),
        ((sweeps, 2, nz, ra, rank), F32),
        ((sweeps, nz, ra, rank), F32),
        ((sweeps, nz, ra, rank), F32),
        ((sweeps, nz, ra, rank), F32),
        ((sweeps, nr, rb, rank), F32),
        ((sweeps, nr, rb, rank), F32),
        ((sweeps, nr, 2, slots * depth, rank), F32),
        ((nr, 2, tags, rank), F32),
        ((sweeps, nzc, rc, rank), F32),
        ((sweeps, nz, rc, rank), F32),
        ((sweeps, 2, nr, rank // nr // 2, rank), F32),
        ((sweeps, nr, rank // nr // 2, rank), F32),
        ((sweeps, 2, nr, rank // nr // 2, rank), F32),
        ((sweeps, nr, 2, rank // nr // 2, rank), F32),
        ((sweeps, rank // nr // 2, rank), F32),
        ((sweeps, nz, rank // nr // 2, rank), F32),
        ((sweeps, nr, 2, rank // nr // 2, rank), F32),
    ]
    new_a, new_b, new_c = pl.pallas_call(
        functools.partial(kernel, nr, nc, sems),
        out_shape=(
            jax.ShapeDtypeStruct((ra, rank), F32),
            jax.ShapeDtypeStruct((rb, rank), F32),
            jax.ShapeDtypeStruct((nr, 2, nzc, rc, rank), F32),
        ),
        in_specs=[smem, smem, smem] + [far] * 4,
        out_specs=(vmem, vmem, vmem),
        scratch_shapes=[
            [pltpu.VMEM(*each) for each in one] if isinstance(one, list) else pltpu.VMEM(*one)
            for one in scratch
        ]
        + [pltpu.SemaphoreType.DMA((4,)), pltpu.SemaphoreType.DMA((sems,)), pltpu.SemaphoreType.DMA((sems,))],
        compiler_params=pltpu.CompilerParams(
            collective_id=0, has_side_effects=True, vmem_limit_bytes=64 * 1024 * 1024 - 256 * 1024
        ),
        name="sweeps",
    )(
        jnp.swapaxes(brick_coords, 2, 3), brick_counts, step_sizes,
        bricks.reshape(slots, depth, tile, tile), init_a[0], init_b[0], init_c,
    )
    return new_a[None], new_b[None], new_c.reshape(depth_c, rank)


def solution(mesh):
    placed = (
        P("row", "col", None, None, None, None),
        P("row", "col", None, None),
        P("row", "col"),
        P(),
        P("row", "col", None),
        P("col", "row", None),
        P(),
    )
    return jax.shard_map(
        functools.partial(shards, mesh.shape["row"], mesh.shape["col"]),
        mesh=mesh,
        in_specs=placed,
        out_specs=(P("row", "col", None), P("col", "row", None), P()),
        check_vma=False,
    )
```

time: 75.7 us -> 65.3 us (0.86)
  Pallas kernels: 66.5 us -> 59.7 us
  local copies, waits for them, and re-layouts: 7.63 us -> 4.01 us
    pallas_call x1, Pallas kernels: 66.5 us -> 59.7 us  [shards(): pl.pallas_call(functools.partial(kernel, nr, nc, sems), out_shape=(jax.Sh...]
    unnamed x15 -> x5, local copies, waits for them, and re-layouts: 7.28 us -> 4.01 us
where the time goes in v2:
time: 65.3 us; the launch traced here: 65 us
  Pallas kernels  59.7 us (91%)
  local copies, waits for them, and re-layouts  4.01 us (6%)
  between operations  1.29 us (2%)
    pallas_call x1, Pallas kernels, shards(): pl.pallas_call(functools.partial(kernel, nr, nc, sems), out_shape=(jax.Sh...  59.7 us
    unnamed x5, local copies, waits for them, and re-layouts  4.01 us

profile of v2, /device:TPU:1, one launch (start us, length us, event | category | flops | bytes accessed | tf_op | source)
XLA Modules:
  0.0 65.0 jit_solution(12375616962031666037)
XLA Ops:
  1.3 59.7 %sweeps.1 = (f32[64,256]{1,0:T(8,128)}, f32[64,256]{1,0:T(8,128)}, f32[4,2,4,16,256]{4,3,2,1,0:T(8,128)}) custom-call(s32[1,1,2,3]{3,2,1,0:T(2,128)} %bitcast.13, s32[1,1]{1,0:T(1,128)S(6)} %copy.13.counts, f32[2,3]{1,0:T(2,128)} %rates.1, bf16[2,16,128,128]{3,2,1,0:T(8,128)(2,1)} %bitcast.7, f32[64,256]{1,0:T(8,128)} %bitcast.9, f32[64,256]{1,0:T(8,128)} %bitcast.10, ...), custom_call_target="tpu_custom_call" | custom-call | tf_op jit(solution)/shard_map/sweeps/pallas_call | solution.py:461
  61.0 0.0 copy-start
  61.0 1.5 %copy.14 = f32[1,64,256]{2,1,0:T(8,128)} copy(f32[1,64,256]{2,1,0:T(8,128)} %bitcast.12) | data formatting | bytes 131072
  62.5 0.0 copy-done
  62.5 0.6 copy.15
  63.2 1.9 %copy.16 = f32[512,256]{1,0:T(8,128)} copy(f32[512,256]{1,0:T(8,128)} %bitcast.8) | data formatting | bytes 1048576
Async XLA Ops:
  61.0 1.5 %copy-start = (f32[64,256]{1,0:T(8,128)S(1)}, f32[64,256]{1,0:T(8,128)}, u32[]{:S(2)}) copy-start(f32[64,256]{1,0:T(8,128)} %get-tuple-element.7) | copy-start | bytes 196612

commit v3 on v2

--- a/solution.py
+++ b/solution.py
@@ -10,6 +10,7 @@
 MESH = pl.DeviceIdType.MESH
 F32 = jnp.float32
 BF16 = jnp.bfloat16
+VMEM_BYTES = 64 * 1024 * 1024 - 256 * 1024
 
 
 def gram(values):
@@ -23,11 +24,11 @@
     places, counts, rates, far_bricks, far_a0, far_b0, far_c0,
     out_a, out_b, out_c,
     bricks, init_a, init_b, init_c,
-    flip, a_all, b_all, c_all, acc_a, acc_b, spread,
+    flip, a_all, b_all, c_all, acc_a, acc_b, spread, deep_all, final_c,
     da, da1, da_sum, da2, db, db2,
     cc, tags, csum, c3,
     sa_part, sa1, sa_full, sb_part, sb1, sb2, sb_full,
-    load, send, recv,
+    load, store, send, recv,
 ):
     nz = nc // 2
     slots, depth, tile, _ = bricks.shape
@@ -202,115 +203,90 @@
     strip = 8
     batch = 4
 
-    def fill(value_at, right):
+    def fill(wide, value_at, right):
         for k in range(0, depth, batch):
-            spread[k * tile:(k + batch) * tile, :] = jnp.dot(
+            wide[k * tile:(k + batch) * tile, :] = jnp.dot(
                 value_at(k).reshape(batch * tile, tile), right, preferred_element_type=F32
             )
 
-    def wide_pass(s, slot):
-        fill(lambda k: bricks[slot, k:k + batch], tile_b(s, slot))
-        c_rows = rows_c(s, slot)
-        acc_b[slot] = tile_a(s, slot).astype(F32)
-
-        def body(at, carry):
-            low = pl.multiple_of(at * strip, strip)
-            a_rows = acc_b[slot, pl.ds(low, strip), :]
-            sums = jnp.zeros((strip, rank), F32)
-            along_c = []
-            for k in range(depth):
-                part = spread[pl.ds(pl.multiple_of(k * tile + low, strip), strip), :]
-                sums = sums + part * c_rows[k:k + 1]
-                along_c.append(carry[k] + part * a_rows)
-            acc_a[slot, pl.ds(low, strip), :] = sums
-            return tuple(along_c)
-
-        empty = tuple(jnp.zeros((strip, rank), F32) for _ in range(depth))
-        along_c = lax.fori_loop(0, tile // strip, body, empty)
-        cc[s, r, core, slot * depth:(slot + 1) * depth, :] = jnp.concatenate(
-            [jnp.sum(one, axis=0, keepdims=True) for one in along_c], axis=0
-        )
-
-    def deep_pass(s, slot):
-        fill(lambda k: flip[slot, k:k + batch], tile_a(s, slot))
-        c_rows = rows_c(s, slot)
-
+    def weigh(wide, c_rows, result):
         def body(at, carry):
             low = pl.multiple_of(at * strip, strip)
             sums = jnp.zeros((strip, rank), F32)
             for k in range(depth):
-                part = spread[pl.ds(pl.multiple_of(k * tile + low, strip), strip), :]
+                part = wide[pl.ds(pl.multiple_of(k * tile + low, strip), strip), :]
                 sums = sums + part * c_rows[k:k + 1]
-            acc_b[slot, pl.ds(low, strip), :] = sums
+            result[pl.ds(low, strip), :] = sums
             return carry
 
         lax.fori_loop(0, tile // strip, body, 0)
 
-    far_b = send_b(0)
-    near_a, far_a = send_a(0)
-    far_tags = spread_chips(tags.at[r, core])
-    loads[2].wait()
-    mine = z if nzc > 1 else 0
-    start_c = r * k_row + core * k_half + mine * (k_half // nzc)
-    state_c = init_c[pl.ds(pl.multiple_of(start_c, 8), k_half // nzc), :]
-    c_all[0][...] = init_c[...].astype(BF16).reshape(c_all[0].shape)
-    gram_c = gram(c_all[0][...].reshape(nr * k_row, rank))
-    loads[3].wait()
-    wait_c = []
-
-    for s in range(sweeps):
-        done(far_b)
-        sb_part[s] = gram(b_all[s][...].reshape(nr * rb, rank)).reshape(sb_part.shape[1:])
-        step_sb1 = to_core(sb_part.at[s, r, other], sb1.at[s])
-        passed_a = forward_a(s, far_a)
-        step_sb1.wait_recv()
-        sb2[s, z] = sb_part[s, r, core] + sb1[s]
-        step_sb2 = [
-            push(sb2.at[s, z], sb2.at[s, z], r, z_peer(step)[0] * 2 + core)
-            for step in range(1, nz)
-        ]
-        near_a.wait_recv()
-        done(passed_a)
-        sa_part[s] = gram(a_all[s][...].reshape(nc * ra, rank)).reshape(sa_part.shape[1:])
-        sa1[s, r] = sa_part[s, core, r]
-        step_sa1 = [
-            push(sa_part.at[s, core, row_peer(step)[0]], sa1.at[s, r], row_peer(step)[0], c)
-            for step in range(1, nr)
-        ]
-        done(wait_c)
+    def along_c(s, slot):
+        wide = deep_all.at[slot]
+        acc_b[slot] = tile_b(s, slot).astype(F32)
+
+        def body(at, carry):
+            low = pl.multiple_of(at * strip, strip)
+            rows = acc_b[slot, pl.ds(low, strip), :]
+            return tuple(
+                carry[k] + wide[pl.ds(pl.multiple_of(k * tile + low, strip), strip), :] * rows
+                for k in range(depth)
+            )
+
+        empty = tuple(jnp.zeros((strip, rank), F32) for _ in range(depth))
+        found = lax.fori_loop(0, tile // strip, body, empty)
+        cc[s, r, core, slot * depth:(slot + 1) * depth, :] = jnp.concatenate(
+            [jnp.sum(one, axis=0, keepdims=True) for one in found], axis=0
+        )
+
+    def wide_stage(s):
         for slot in range(slots):
-            wide_pass(s, slot)
-        step_c1 = spread_chips(cc.at[s, r, core])
+            fill(spread, lambda k: bricks[slot, k:k + batch], tile_b(s, slot))
+            weigh(spread, rows_c(s, slot), acc_a.at[slot])
+        copies = {}
         for g in range(nc):
             at, off = g // qa, (g % qa) * ra
             da[s, g % 2, g // 2] = sum(
                 w_i[slot][at] * acc_a[slot, off:off + ra, :] for slot in range(slots)
             )
-        step_da1 = {}
         for step in list(range(1, nz)) + [0]:
             to = z_peer(step)[0]
-            step_da1[step] = to_core(da.at[s, other, to], da1.at[s, to])
-
-        done(step_sa1)
-        sa_full[s, core, r] = total(sa1, s, nr)
-        step_sa2 = spread_row(lambda at: sa_full.at[s, core, at])
-        done(step_sb2)
-        sb_full[s, r, core] = total(sb2, s, nz)
-        step_sb3 = spread_row(lambda at: sb_full.at[s, at, core])
-
-        step_da2 = []
+            copies[step] = to_core(da.at[s, other, to], da1.at[s, to])
+        return copies
+
+    def deep_stage(s):
+        for slot in range(slots):
+            fill(deep_all.at[slot], lambda k: flip[slot, k:k + batch], tile_a(s, slot))
+            along_c(s, slot)
+        return spread_chips(cc.at[s, r, core])
+
+    def drive_b_stage(s):
+        for slot in range(slots):
+            weigh(deep_all.at[slot], rows_c(s, slot), acc_b.at[slot])
+        for g in range(nr):
+            at, off = g // qb, (g % qb) * rb
+            db[s, g] = sum(
+                w_j[slot][at] * acc_b[slot, off:off + rb, :] for slot in range(slots)
+            )
+        db2[s, r] = db[s, r]
+        return [
+            push(db.at[s, row_peer(step)[0]], db2.at[s, r], row_peer(step)[0], c)
+            for step in range(1, nr)
+        ]
+
+    def drive_a_stage(s, arriving):
+        copies = []
         for step in list(range(1, nz)) + [0]:
             to = z_peer(step)[0]
-            step_da1[step].wait_recv()
+            arriving[step].wait_recv()
             if step == 0:
                 da2[s, z] = da[s, core, z] + da1[s, z]
             else:
                 da_sum[s, to] = da[s, core, to] + da1[s, to]
-                step_da2.append(push(da_sum.at[s, to], da2.at[s, z], r, to * 2 + core))
-
-        done(step_c1)
-        if s == 0:
-            done(far_tags)
+                copies.append(push(da_sum.at[s, to], da2.at[s, z], r, to * 2 + core))
+        return copies
+
+    def drive_c_stage(s):
         half = spots // 2
         found = []
         for one in range(half):
@@ -325,91 +301,195 @@
             found.append(sums)
         csum[s] = jnp.concatenate(found, axis=0).reshape(csum.shape[1:])
         c3[s, z] = csum[s, mine]
-        step_c3 = []
+        copies = []
         for step in range(1, nz):
             to = z_peer(step)[0]
-            step_c3.append(
+            copies.append(
                 push(csum.at[s, to if nzc > 1 else 0], c3.at[s, z], r, to * 2 + core)
             )
-
-        for slot in range(slots):
-            if s == 0:
-                turn(slot)
-            deep_pass(s, slot)
-        for g in range(nr):
-            at, off = g // qb, (g % qb) * rb
-            db[s, g] = sum(
-                w_j[slot][at] * acc_b[slot, off:off + rb, :] for slot in range(slots)
-            )
-        db2[s, r] = db[s, r]
-        step_db = [
-            push(db.at[s, row_peer(step)[0]], db2.at[s, r], row_peer(step)[0], c)
+        return copies
+
+    def gram_b_stage(s):
+        sb_part[s] = gram(b_all[s][...].reshape(nr * rb, rank)).reshape(sb_part.shape[1:])
+        return to_core(sb_part.at[s, r, other], sb1.at[s])
+
+    def pair_b_stage(s, arriving):
+        arriving.wait_recv()
+        sb2[s, z] = sb_part[s, r, core] + sb1[s]
+        return [
+            push(sb2.at[s, z], sb2.at[s, z], r, z_peer(step)[0] * 2 + core)
+            for step in range(1, nz)
+        ]
+
+    def gram_a_stage(s):
+        sa_part[s] = gram(a_all[s][...].reshape(nc * ra, rank)).reshape(sa_part.shape[1:])
+        sa1[s, r] = sa_part[s, core, r]
+        return [
+            push(sa_part.at[s, core, row_peer(step)[0]], sa1.at[s, r], row_peer(step)[0], c)
             for step in range(1, nr)
         ]
 
+    def prepare(state, hess):
+        scale = jnp.sum(jnp.abs(hess), axis=0, keepdims=True) + 1e-06
+        high = hess.astype(BF16)
+        low = (hess - high.astype(F32)).astype(BF16)
+        top = state.astype(BF16)
+        rest = (state - top.astype(F32)).astype(BF16)
+        rows = state.shape[0]
+        both = jnp.dot(
+            jnp.concatenate([top, rest], axis=0), high, preferred_element_type=F32
+        )
+        moved = both[:rows] + both[rows:] + jnp.dot(top, low, preferred_element_type=F32)
+        return moved, scale
+
+    def finish(state, ready, drive, rate):
+        moved, scale = ready
+        return jnp.maximum(state - rate * (moved - drive) / scale, 0.0)
+
+    stored = []
+
+    def keep(src, dst):
+        copy = pltpu.make_async_copy(src, dst, store.at[len(stored)])
+        copy.start()
+        stored.append(copy)
+
+    far_b = send_b(0)
+    near_a, far_a = send_a(0)
+    far_tags = spread_chips(tags.at[r, core])
+    loads[2].wait()
+    mine = z if nzc > 1 else 0
+    start_c = r * k_row + core * k_half + mine * (k_half // nzc)
+    state_c = init_c[pl.ds(pl.multiple_of(start_c, 8), k_half // nzc), :]
+    c_all[0][...] = init_c[...].astype(BF16).reshape(c_all[0].shape)
+    gram_c = gram(c_all[0][...].reshape(nr * k_row, rank))
+    loads[3].wait()
+    for slot in range(slots):
+        turn(slot)
+    far_c = []
+
+    for s in range(sweeps):
+        last = s == sweeps - 1
+        done(far_b)
+        step_sb1 = gram_b_stage(s)
+        if s == 0:
+            step_da1 = wide_stage(s)
+            step_sb2 = pair_b_stage(s, step_sb1)
+            passed_a = forward_a(s, far_a)
+            step_da2 = drive_a_stage(s, step_da1)
+            near_a.wait_recv()
+            done(passed_a)
+            step_c1 = deep_stage(s)
+            step_sa1 = gram_a_stage(s)
+            step_db = drive_b_stage(s)
+            done(step_sb2)
+            sb_full[s, r, core] = total(sb2, s, nz)
+            step_sb3 = spread_row(lambda at: sb_full.at[s, at, core])
+            done(step_sa1)
+            sa_full[s, core, r] = total(sa1, s, nr)
+            step_sa2 = spread_row(lambda at: sa_full.at[s, core, at])
+            done(far_tags)
+            done(step_c1)
+            step_c3 = drive_c_stage(s)
+        else:
+            passed_a = forward_a(s, far_a)
+            step_sb2 = pair_b_stage(s, step_sb1)
+            done(far_c)
+            wait_c = spread_chips(c_all[s].at[r, core])
+            near_a.wait_recv()
+            done(passed_a)
+            step_c1 = deep_stage(s)
+            step_sa1 = gram_a_stage(s)
+            done(wait_c)
+            step_da1 = wide_stage(s)
+            done(step_sb2)
+            sb_full[s, r, core] = total(sb2, s, nz)
+            step_sb3 = spread_row(lambda at: sb_full.at[s, at, core])
+            done(step_sa1)
+            sa_full[s, core, r] = total(sa1, s, nr)
+            step_sa2 = spread_row(lambda at: sa_full.at[s, core, at])
+            done(step_c1)
+            step_c3 = drive_c_stage(s)
+            step_da2 = drive_a_stage(s, step_da1)
+            gram_c = gram(c_all[s][...].reshape(nr * k_row, rank))
+            step_db = drive_b_stage(s)
+        step_sb4 = forward_row(lambda at: sb_full.at[s, at, core], step_sb3)
         step_sa3 = forward_row(lambda at: sa_full.at[s, core, at], step_sa2)
-        step_sb4 = forward_row(lambda at: sb_full.at[s, at, core], step_sb3)
-
-        def prepare(state, hess):
-            scale = jnp.sum(jnp.abs(hess), axis=0, keepdims=True) + 1e-06
-            high = hess.astype(BF16)
-            low = (hess - high.astype(F32)).astype(BF16)
-            top = state.astype(BF16)
-            rest = (state - top.astype(F32)).astype(BF16)
-            rows = state.shape[0]
-            both = jnp.dot(
-                jnp.concatenate([top, rest], axis=0), high, preferred_element_type=F32
-            )
-            moved = both[:rows] + both[rows:] + jnp.dot(top, low, preferred_element_type=F32)
-            return moved, scale
-
-        def finish(state, ready, drive, rate):
-            moved, scale = ready
-            return jnp.maximum(state - rate * (moved - drive) / scale, 0.0)
-
-        last = s == sweeps - 1
-        done(step_sa3)
-        gram_a = sa_full[s].reshape(rank, rank)
         done(step_sb4)
         gram_b = sb_full[s].reshape(rank, rank)
-        ready_c = prepare(state_c, gram_a * gram_b)
-        done(step_c3)
-        state_c = finish(state_c, ready_c, total(c3, s, nz), rates[s, 2])
-        if last:
-            out_c[r, core, mine] = state_c
-            far_c = spread_c(lambda at: out_c.at[r, core, at])
-        else:
+        if not last:
+            ready_a = prepare(state_a, gram_b * gram_c)
+            done(step_da2)
+            state_a = finish(state_a, ready_a, total(da2, s, nz), rates[s, 0])
+            a_all[s + 1][c] = state_a.astype(BF16)
+            near_a, far_a = send_a(s + 1)
+            done(step_sa3)
+            gram_a = sa_full[s].reshape(rank, rank)
+            ready_b = prepare(state_b, gram_a * gram_c)
+            done(step_db)
+            state_b = finish(state_b, ready_b, total(db2, s, nr), rates[s, 1])
+            b_all[s + 1][r] = state_b.astype(BF16)
+            far_b = send_b(s + 1)
+            ready_c = prepare(state_c, gram_a * gram_b)
+            done(step_c3)
+            state_c = finish(state_c, ready_c, total(c3, s, nz), rates[s, 2])
             c_all[s + 1][r, core, mine] = state_c.astype(BF16)
             far_c = spread_c(lambda at: c_all[s + 1].at[r, core, at])
-        ready_b = prepare(state_b, gram_a * gram_c)
-        done(step_db)
-        state_b = finish(state_b, ready_b, total(db2, s, nr), rates[s, 1])
-        if last:
-            out_b[...] = state_b
         else:
-            b_all[s + 1][r] = state_b.astype(BF16)
-            far_b = send_b(s + 1)
-        done(far_c)
-        if last:
-            far_c = spread_row(lambda at: out_c.at[at, core])
-        else:
-            wait_c = spread_chips(c_all[s + 1].at[r, core])
-        ready_a = prepare(state_a, gram_b * gram_c)
-        done(step_da2)
-        state_a = finish(state_a, ready_a, total(da2, s, nz), rates[s, 0])
-        if last:
-            out_a[...] = state_a
-            done(forward_row(lambda at: out_c.at[at, core], far_c))
-        else:
-            a_all[s + 1][c] = state_a.astype(BF16)
-            near_a, far_a = send_a(s + 1)
-            done(wait_c)
-            wait_c = []
-            gram_c = gram(c_all[s + 1][...].reshape(nr * k_row, rank))
-
+            done(step_sa3)
+            gram_a = sa_full[s].reshape(rank, rank)
+            ready_c = prepare(state_c, gram_a * gram_b)
+            done(step_c3)
+            final_c[r, core, mine] = finish(state_c, ready_c, total(c3, s, nz), rates[s, 2])
+            far_c = spread_c(lambda at: final_c.at[r, core, at])
+            ready_b = prepare(state_b, gram_a * gram_c)
+            ready_a = prepare(state_a, gram_b * gram_c)
+            done(far_c)
+            far_c = spread_row(lambda at: final_c.at[at, core])
+            done(step_db)
+            init_b[...] = finish(state_b, ready_b, total(db2, s, nr), rates[s, 1])
+            keep(init_b, out_b)
+            done(step_da2)
+            init_a[...] = finish(state_a, ready_a, total(da2, s, nz), rates[s, 0])
+            keep(init_a, out_a)
+            passed_c = forward_row(lambda at: final_c.at[at, core], far_c)
+            for step in range(nr):
+                at = row_peer(step)[1]
+                keep(final_c.at[at, core], out_c.at[at, core])
+            for step in range(nr):
+                passed_c[step].wait_recv()
+                at = row_peer(step)[1]
+                keep(final_c.at[at, other], out_c.at[at, other])
+
+    for copy in stored:
+        copy.wait()
     for copy in started:
         copy.wait_send()
     assert used[0] <= sems_of
+
+
+def hand_out(*arrays):
+    count = len(arrays)
+
+    def copy_all(*refs):
+        copies = [
+            pltpu.make_async_copy(refs[at], refs[count + at], refs[-1].at[at])
+            for at in range(count)
+        ]
+        for copy in copies:
+            copy.start()
+        for copy in copies:
+            copy.wait()
+
+    far = pl.BlockSpec(memory_space=pltpu.HBM)
+    return pl.pallas_call(
+        copy_all,
+        out_shape=tuple(jax.ShapeDtypeStruct(one.shape, one.dtype) for one in arrays),
+        in_specs=[far] * count,
+        out_specs=(far,) * count,
+        scratch_shapes=[pltpu.SemaphoreType.DMA((count,))],
+        compiler_params=pltpu.CompilerParams(vmem_limit_bytes=VMEM_BYTES),
+        name="hand_out",
+    )(*arrays)
 
 
 def shards(nr, nc, bricks, brick_coords, brick_counts, step_sizes, init_a, init_b, init_c):
@@ -425,7 +505,6 @@
     rc = k_half // nzc
     tags = -(-slots // 8) * 8
     sems = 2 * nr + sweeps * (6 * nz + 13 * nr)
-    vmem = pl.BlockSpec(memory_space=pltpu.VMEM)
     smem = pl.BlockSpec(memory_space=pltpu.SMEM)
     far = pl.BlockSpec(memory_space=pltpu.HBM)
     scratch = [
@@ -440,6 +519,8 @@
         ((slots, tile, rank), F32),
         ((slots, tile, rank), F32),
         ((depth * tile, rank), F32),
+        ((slots, depth * tile, rank), F32),
+        ((nr, 2, nzc, rc, rank), F32),
         ((sweeps, 2, nz, ra, rank), F32),
         ((sweeps, nz, ra, rank), F32),
         ((sweeps, nz, ra, rank), F32),
@@ -466,21 +547,21 @@
             jax.ShapeDtypeStruct((nr, 2, nzc, rc, rank), F32),
         ),
         in_specs=[smem, smem, smem] + [far] * 4,
-        out_specs=(vmem, vmem, vmem),
+        out_specs=(far, far, far),
         scratch_shapes=[
             [pltpu.VMEM(*each) for each in one] if isinstance(one, list) else pltpu.VMEM(*one)
             for one in scratch
         ]
-        + [pltpu.SemaphoreType.DMA((4,)), pltpu.SemaphoreType.DMA((sems,)), pltpu.SemaphoreType.DMA((sems,))],
+        + [pltpu.SemaphoreType.DMA((4,)), pltpu.SemaphoreType.DMA((2 + 2 * nr,)), pltpu.SemaphoreType.DMA((sems,)), pltpu.SemaphoreType.DMA((sems,))],
         compiler_params=pltpu.CompilerParams(
-            collective_id=0, has_side_effects=True, vmem_limit_bytes=64 * 1024 * 1024 - 256 * 1024
+            collective_id=0, has_side_effects=True, vmem_limit_bytes=VMEM_BYTES
         ),
         name="sweeps",
     )(
         jnp.swapaxes(brick_coords, 2, 3), brick_counts, step_sizes,
         bricks.reshape(slots, depth, tile, tile), init_a[0], init_b[0], init_c,
     )
-    return new_a[None], new_b[None], new_c.reshape(depth_c, rank)
+    return hand_out(new_a[None], new_b[None], new_c.reshape(depth_c, rank))
 
 
 def solution(mesh):

time: 65.3 us -> 84.2 us (1.29)
  Pallas kernels: 59.7 us -> 82.7 us
  local copies, waits for them, and re-layouts: 4.01 us -> 0 us
    pallas_call x0 -> x1, Pallas kernels: none -> 21 us  [hand_out(): pl.pallas_call(copy_all, out_shape=tuple((jax.ShapeDtypeStruct(one.shape,...]
    unnamed x5 -> x0, local copies, waits for them, and re-layouts: 4.01 us -> none
    pallas_call x1, Pallas kernels: 59.7 us -> 61.8 us  [shards(): pl.pallas_call(functools.partial(kernel, nr, nc, sems), out_shape=(jax.Sh...]
where the time goes in v3:
time: 84.2 us; the launch traced here: 84 us
  Pallas kernels  82.7 us (98%)
  between operations  1.29 us (2%)
    pallas_call x1, Pallas kernels, shards(): pl.pallas_call(functools.partial(kernel, nr, nc, sems), out_shape=(jax.Sh...  61.8 us
    pallas_call x1, Pallas kernels, hand_out(): pl.pallas_call(copy_all, out_shape=tuple((jax.ShapeDtypeStruct(one.shape,...  21 us

profile of v3, /device:TPU:1, one launch (start us, length us, event | category | flops | bytes accessed | tf_op | source)
XLA Modules:
  0.0 84.0 jit_solution(11709456657521613762)
XLA Ops:
  1.3 61.8 %sweeps.1 = (f32[64,256]{1,0:T(8,128)}, f32[64,256]{1,0:T(8,128)}, f32[4,2,4,16,256]{4,3,2,1,0:T(8,128)}) custom-call(s32[1,1,2,3]{3,2,1,0:T(2,128)} %bitcast.13, s32[1,1]{1,0:T(1,128)S(6)} %copy.10.counts, f32[2,3]{1,0:T(2,128)} %rates.1, bf16[2,16,128,128]{3,2,1,0:T(8,128)(2,1)} %bitcast.7, f32[64,256]{1,0:T(8,128)} %bitcast.9, f32[64,256]{1,0:T(8,128)} %bitcast.10, ...), custom_call_target="tpu_custom_call" | custom-call | tf_op jit(solution)/shard_map/sweeps/pallas_call | solution.py:542
  63.1 21.0 %hand_out.1 = (f32[1,64,256]{2,1,0:T(8,128)}, f32[1,64,256]{2,1,0:T(8,128)}, f32[512,256]{1,0:T(8,128)}) custom-call(f32[1,64,256]{2,1,0:T(8,128)} %bitcast.11, f32[1,64,256]{2,1,0:T(8,128)} %bitcast.12, f32[512,256]{1,0:T(8,128)} %bitcast.8), custom_call_target="tpu_custom_call" | custom-call | tf_op jit(solution)/shard_map/hand_out/pallas_call | solution.py:484

commit v4 on v3

--- a/solution.py
+++ b/solution.py
@@ -28,7 +28,7 @@
     da, da1, da_sum, da2, db, db2,
     cc, tags, csum, c3,
     sa_part, sa1, sa_full, sb_part, sb1, sb2, sb_full,
-    load, store, send, recv,
+    load, send, recv,
 ):
     nz = nc // 2
     slots, depth, tile, _ = bricks.shape
@@ -82,10 +82,7 @@
     barrier = pltpu.get_barrier_semaphore()
     pl.semaphore_signal(barrier, inc=1, device_id=(r, z * 2 + other), device_id_type=MESH)
     for step in range(1, nr):
-        for col in (c, z * 2 + other):
-            pl.semaphore_signal(
-                barrier, inc=1, device_id=(row_peer(step)[0], col), device_id_type=MESH
-            )
+        pl.semaphore_signal(barrier, inc=1, device_id=(row_peer(step)[0], c), device_id_type=MESH)
     for step in range(1, nz):
         pl.semaphore_signal(
             barrier, inc=1, device_id=(r, z_peer(step)[0] * 2 + core), device_id_type=MESH
@@ -113,52 +110,30 @@
     for slot in range(slots):
         mark = jnp.where(live[slot], spot_k[slot], -1).astype(F32)
         tag = jnp.where(number == slot, mark, tag)
-    tags[r, core] = tag
+    tags[core, r] = tag
 
     loads[0].wait()
     state_b = init_b[...]
     b_all[0][r] = state_b.astype(BF16)
     loads[1].wait()
     state_a = init_a[...]
-    a_all[0][c] = state_a.astype(BF16)
-
-    pl.semaphore_wait(barrier, 1 + 2 * (nr - 1) + (nz - 1))
+    a_all[0][core, z] = state_a.astype(BF16)
+
+    pl.semaphore_wait(barrier, 1 + (nr - 1) + (nz - 1))
 
     def send_b(s):
         return [push(b_all[s].at[r], b_all[s].at[r], row_peer(step)[0], c) for step in range(1, nr)]
 
     def send_a(s):
-        near = to_core(a_all[s].at[c], a_all[s].at[c])
-        return near, [
-            push(a_all[s].at[c], a_all[s].at[c], r, z_peer(step)[0] * 2 + core)
-            for step in range(1, nz)
-        ]
-
-    def forward_a(s, far):
-        passed = []
-        for step in range(1, nz):
-            far[step - 1].wait_recv()
-            at = z_peer(step)[1] * 2 + core
-            passed.append(to_core(a_all[s].at[at], a_all[s].at[at]))
-        return passed
-
-    def forward_row(ref_at, far):
-        passed = [to_core(ref_at(r), ref_at(r))]
-        for step in range(1, nr):
-            far[step - 1].wait_recv()
-            at = row_peer(step)[1]
-            passed.append(to_core(ref_at(at), ref_at(at)))
-        return passed
+        mine_a = a_all[s].at[core, z]
+        return [push(mine_a, mine_a, r, z_peer(step)[0] * 2 + core) for step in range(1, nz)]
+
+    def pass_on(ref, far):
+        done(far)
+        return to_core(ref, ref)
 
     def spread_row(ref_at):
         return [push(ref_at(r), ref_at(r), row_peer(step)[0], c) for step in range(1, nr)]
-
-    def spread_chips(ref):
-        copies = [to_core(ref, ref)]
-        for step in range(1, nr):
-            for col in (c, z * 2 + other):
-                copies.append(push(ref, ref, row_peer(step)[0], col))
-        return copies
 
     def spread_c(ref_at):
         if nzc == 1:
@@ -184,7 +159,9 @@
         lax.fori_loop(0, depth, one, 0, unroll=4)
 
     def tile_a(s, slot):
-        return a_all[s][pl.ds(spot_i[slot] * qa, qa)].reshape(tile, rank)
+        half = qa // 2
+        sides = [a_all[s][side, pl.ds(spot_i[slot] * half, half)] for side in range(2)]
+        return jnp.stack(sides, axis=1).reshape(tile, rank)
 
     def tile_b(s, slot):
         return b_all[s][pl.ds(spot_j[slot] * qb, qb)].reshape(tile, rank)
@@ -193,7 +170,7 @@
         at = spot_k[slot]
         within = lax.rem(at, spots)
         low = lax.rem(within, spots // 2)
-        wide_c = c_all[s][lax.div(at, spots), lax.div(within, spots // 2)]
+        wide_c = c_all[s][lax.div(within, spots // 2), lax.div(at, spots)]
         flat = wide_c.astype(F32).reshape(spots // 2, depth, rank)
         picked = jnp.zeros((depth, rank), F32)
         for one in range(spots // 2):
@@ -235,7 +212,7 @@
 
         empty = tuple(jnp.zeros((strip, rank), F32) for _ in range(depth))
         found = lax.fori_loop(0, tile // strip, body, empty)
-        cc[s, r, core, slot * depth:(slot + 1) * depth, :] = jnp.concatenate(
+        cc[s, core, r, slot * depth:(slot + 1) * depth, :] = jnp.concatenate(
             [jnp.sum(one, axis=0, keepdims=True) for one in found], axis=0
         )
 
@@ -243,22 +220,18 @@
         for slot in range(slots):
             fill(spread, lambda k: bricks[slot, k:k + batch], tile_b(s, slot))
             weigh(spread, rows_c(s, slot), acc_a.at[slot])
-        copies = {}
         for g in range(nc):
             at, off = g // qa, (g % qa) * ra
             da[s, g % 2, g // 2] = sum(
                 w_i[slot][at] * acc_a[slot, off:off + ra, :] for slot in range(slots)
             )
-        for step in list(range(1, nz)) + [0]:
-            to = z_peer(step)[0]
-            copies[step] = to_core(da.at[s, other, to], da1.at[s, to])
-        return copies
+        return to_core(da.at[s, other], da1.at[s])
 
     def deep_stage(s):
         for slot in range(slots):
             fill(deep_all.at[slot], lambda k: flip[slot, k:k + batch], tile_a(s, slot))
             along_c(s, slot)
-        return spread_chips(cc.at[s, r, core])
+        return spread_row(lambda at: cc.at[s, core, at])
 
     def drive_b_stage(s):
         for slot in range(slots):
@@ -276,9 +249,9 @@
 
     def drive_a_stage(s, arriving):
         copies = []
+        arriving.wait_recv()
         for step in list(range(1, nz)) + [0]:
             to = z_peer(step)[0]
-            arriving[step].wait_recv()
             if step == 0:
                 da2[s, z] = da[s, core, z] + da1[s, z]
             else:
@@ -295,8 +268,8 @@
             for src in range(nr):
                 for side in range(2):
                     for slot in range(slots):
-                        term = cc[s, src, side, slot * depth:(slot + 1) * depth, :]
-                        mark = tags[src, side, slot:slot + 1, :]
+                        term = cc[s, side, src, slot * depth:(slot + 1) * depth, :]
+                        mark = tags[side, src, slot:slot + 1, :]
                         sums = sums + jnp.where(mark == want, term, 0.0)
             found.append(sums)
         csum[s] = jnp.concatenate(found, axis=0).reshape(csum.shape[1:])
@@ -344,23 +317,21 @@
 
     def finish(state, ready, drive, rate):
         moved, scale = ready
-        return jnp.maximum(state - rate * (moved - drive) / scale, 0.0)
-
-    stored = []
-
-    def keep(src, dst):
-        copy = pltpu.make_async_copy(src, dst, store.at[len(stored)])
-        copy.start()
-        stored.append(copy)
+        return state - rate * (moved - drive) / scale
 
     far_b = send_b(0)
-    near_a, far_a = send_a(0)
-    far_tags = spread_chips(tags.at[r, core])
+    far_a = send_a(0)
+    far_tags = spread_row(lambda at: tags.at[core, at])
     loads[2].wait()
     mine = z if nzc > 1 else 0
     start_c = r * k_row + core * k_half + mine * (k_half // nzc)
     state_c = init_c[pl.ds(pl.multiple_of(start_c, 8), k_half // nzc), :]
-    c_all[0][...] = init_c[...].astype(BF16).reshape(c_all[0].shape)
+    for at in range(nr):
+        for side in range(2):
+            low = at * k_row + side * k_half
+            c_all[0][side, at] = init_c[low:low + k_half, :].astype(BF16).reshape(
+                c_all[0].shape[2:]
+            )
     gram_c = gram(c_all[0][...].reshape(nr * k_row, rank))
     loads[3].wait()
     for slot in range(slots):
@@ -369,127 +340,94 @@
 
     for s in range(sweeps):
         last = s == sweeps - 1
+        first = s == 0
         done(far_b)
         step_sb1 = gram_b_stage(s)
-        if s == 0:
+        if first:
             step_da1 = wide_stage(s)
-            step_sb2 = pair_b_stage(s, step_sb1)
-            passed_a = forward_a(s, far_a)
+        near_a = pass_on(a_all[s].at[core], far_a)
+        step_sb2 = pair_b_stage(s, step_sb1)
+        if first:
             step_da2 = drive_a_stage(s, step_da1)
-            near_a.wait_recv()
-            done(passed_a)
-            step_c1 = deep_stage(s)
-            step_sa1 = gram_a_stage(s)
-            step_db = drive_b_stage(s)
-            done(step_sb2)
-            sb_full[s, r, core] = total(sb2, s, nz)
-            step_sb3 = spread_row(lambda at: sb_full.at[s, at, core])
-            done(step_sa1)
-            sa_full[s, core, r] = total(sa1, s, nr)
-            step_sa2 = spread_row(lambda at: sa_full.at[s, core, at])
-            done(far_tags)
-            done(step_c1)
-            step_c3 = drive_c_stage(s)
         else:
-            passed_a = forward_a(s, far_a)
-            step_sb2 = pair_b_stage(s, step_sb1)
             done(far_c)
-            wait_c = spread_chips(c_all[s].at[r, core])
-            near_a.wait_recv()
-            done(passed_a)
-            step_c1 = deep_stage(s)
-            step_sa1 = gram_a_stage(s)
-            done(wait_c)
+            far_c = spread_row(lambda at: c_all[s].at[core, at])
+        near_a.wait_recv()
+        step_c1 = deep_stage(s)
+        step_sa1 = gram_a_stage(s)
+        if first:
+            near_tags = pass_on(tags.at[core], far_tags)
+        else:
+            near_c = pass_on(c_all[s].at[core], far_c)
+        near_cc = pass_on(cc.at[s, core], step_c1)
+        if not first:
+            near_c.wait_recv()
             step_da1 = wide_stage(s)
-            done(step_sb2)
-            sb_full[s, r, core] = total(sb2, s, nz)
-            step_sb3 = spread_row(lambda at: sb_full.at[s, at, core])
-            done(step_sa1)
-            sa_full[s, core, r] = total(sa1, s, nr)
-            step_sa2 = spread_row(lambda at: sa_full.at[s, core, at])
-            done(step_c1)
-            step_c3 = drive_c_stage(s)
+        done(step_sa1)
+        sa_full[s, core, r] = total(sa1, s, nr)
+        step_sa2 = spread_row(lambda at: sa_full.at[s, core, at])
+        done(step_sb2)
+        sb_full[s, core, r] = total(sb2, s, nz)
+        step_sb3 = spread_row(lambda at: sb_full.at[s, core, at])
+        if first:
+            near_tags.wait_recv()
+        near_cc.wait_recv()
+        step_c3 = drive_c_stage(s)
+        if not first:
             step_da2 = drive_a_stage(s, step_da1)
             gram_c = gram(c_all[s][...].reshape(nr * k_row, rank))
-            step_db = drive_b_stage(s)
-        step_sb4 = forward_row(lambda at: sb_full.at[s, at, core], step_sb3)
-        step_sa3 = forward_row(lambda at: sa_full.at[s, core, at], step_sa2)
-        done(step_sb4)
-        gram_b = sb_full[s].reshape(rank, rank)
+        step_db = drive_b_stage(s)
+        near_sa = pass_on(sa_full.at[s, core], step_sa2)
+        near_sb = pass_on(sb_full.at[s, core], step_sb3)
+        near_sb.wait_recv()
+        gram_b = jnp.stack([sb_full[s, side] for side in range(2)], axis=1).reshape(rank, rank)
         if not last:
             ready_a = prepare(state_a, gram_b * gram_c)
             done(step_da2)
-            state_a = finish(state_a, ready_a, total(da2, s, nz), rates[s, 0])
-            a_all[s + 1][c] = state_a.astype(BF16)
-            near_a, far_a = send_a(s + 1)
-            done(step_sa3)
+            state_a = jnp.maximum(finish(state_a, ready_a, total(da2, s, nz), rates[s, 0]), 0.0)
+            a_all[s + 1][core, z] = state_a.astype(BF16)
+            far_a = send_a(s + 1)
+            near_sa.wait_recv()
             gram_a = sa_full[s].reshape(rank, rank)
             ready_b = prepare(state_b, gram_a * gram_c)
             done(step_db)
-            state_b = finish(state_b, ready_b, total(db2, s, nr), rates[s, 1])
+            state_b = jnp.maximum(finish(state_b, ready_b, total(db2, s, nr), rates[s, 1]), 0.0)
             b_all[s + 1][r] = state_b.astype(BF16)
             far_b = send_b(s + 1)
             ready_c = prepare(state_c, gram_a * gram_b)
             done(step_c3)
-            state_c = finish(state_c, ready_c, total(c3, s, nz), rates[s, 2])
-            c_all[s + 1][r, core, mine] = state_c.astype(BF16)
-            far_c = spread_c(lambda at: c_all[s + 1].at[r, core, at])
+            state_c = jnp.maximum(finish(state_c, ready_c, total(c3, s, nz), rates[s, 2]), 0.0)
+            c_all[s + 1][core, r, mine] = state_c.astype(BF16)
+            far_c = spread_c(lambda at: c_all[s + 1].at[core, r, at])
         else:
-            done(step_sa3)
+            near_sa.wait_recv()
             gram_a = sa_full[s].reshape(rank, rank)
             ready_c = prepare(state_c, gram_a * gram_b)
             done(step_c3)
-            final_c[r, core, mine] = finish(state_c, ready_c, total(c3, s, nz), rates[s, 2])
-            far_c = spread_c(lambda at: final_c.at[r, core, at])
+            final_c[core, r, mine] = finish(state_c, ready_c, total(c3, s, nz), rates[s, 2])
+            far_c = spread_c(lambda at: final_c.at[core, r, at])
             ready_b = prepare(state_b, gram_a * gram_c)
             ready_a = prepare(state_a, gram_b * gram_c)
             done(far_c)
-            far_c = spread_row(lambda at: final_c.at[at, core])
+            far_c = spread_row(lambda at: final_c.at[core, at])
             done(step_db)
-            init_b[...] = finish(state_b, ready_b, total(db2, s, nr), rates[s, 1])
-            keep(init_b, out_b)
+            out_b[...] = finish(state_b, ready_b, total(db2, s, nr), rates[s, 1])
             done(step_da2)
-            init_a[...] = finish(state_a, ready_a, total(da2, s, nz), rates[s, 0])
-            keep(init_a, out_a)
-            passed_c = forward_row(lambda at: final_c.at[at, core], far_c)
-            for step in range(nr):
-                at = row_peer(step)[1]
-                keep(final_c.at[at, core], out_c.at[at, core])
-            for step in range(nr):
-                passed_c[step].wait_recv()
-                at = row_peer(step)[1]
-                keep(final_c.at[at, other], out_c.at[at, other])
-
-    for copy in stored:
-        copy.wait()
+            out_a[...] = finish(state_a, ready_a, total(da2, s, nz), rates[s, 0])
+            near_c = pass_on(final_c.at[core], far_c)
+            for at in range(nr):
+                out_c[at, core] = final_c[core, at]
+            near_c.wait_recv()
+            for at in range(nr):
+                out_c[at, other] = final_c[other, at]
+
     for copy in started:
         copy.wait_send()
     assert used[0] <= sems_of
 
 
-def hand_out(*arrays):
-    count = len(arrays)
-
-    def copy_all(*refs):
-        copies = [
-            pltpu.make_async_copy(refs[at], refs[count + at], refs[-1].at[at])
-            for at in range(count)
-        ]
-        for copy in copies:
-            copy.start()
-        for copy in copies:
-            copy.wait()
-
-    far = pl.BlockSpec(memory_space=pltpu.HBM)
-    return pl.pallas_call(
-        copy_all,
-        out_shape=tuple(jax.ShapeDtypeStruct(one.shape, one.dtype) for one in arrays),
-        in_specs=[far] * count,
-        out_specs=(far,) * count,
-        scratch_shapes=[pltpu.SemaphoreType.DMA((count,))],
-        compiler_params=pltpu.CompilerParams(vmem_limit_bytes=VMEM_BYTES),
-        name="hand_out",
-    )(*arrays)
+def clamp(values):
+    return jnp.maximum(values, 0.0)
 
 
 def shards(nr, nc, bricks, brick_coords, brick_counts, step_sizes, init_a, init_b, init_c):
@@ -507,28 +445,29 @@
     sems = 2 * nr + sweeps * (6 * nz + 13 * nr)
     smem = pl.BlockSpec(memory_space=pltpu.SMEM)
     far = pl.BlockSpec(memory_space=pltpu.HBM)
+    vmem = pl.BlockSpec(memory_space=pltpu.VMEM)
     scratch = [
         ((slots, depth, tile, tile), BF16),
         ((ra, rank), F32),
         ((rb, rank), F32),
         ((depth_c, rank), F32),
         ((slots, depth, tile, tile), BF16),
-        [((nc, ra, rank), BF16)] * sweeps,
+        [((2, nz, ra, rank), BF16)] * sweeps,
         [((nr, rb, rank), BF16)] * sweeps,
-        [((nr, 2, nzc, rc, rank), BF16)] * sweeps,
+        [((2, nr, nzc, rc, rank), BF16)] * sweeps,
         ((slots, tile, rank), F32),
         ((slots, tile, rank), F32),
         ((depth * tile, rank), F32),
         ((slots, depth * tile, rank), F32),
-        ((nr, 2, nzc, rc, rank), F32),
+        ((2, nr, nzc, rc, rank), F32),
         ((sweeps, 2, nz, ra, rank), F32),
         ((sweeps, nz, ra, rank), F32),
         ((sweeps, nz, ra, rank), F32),
         ((sweeps, nz, ra, rank), F32),
         ((sweeps, nr, rb, rank), F32),
         ((sweeps, nr, rb, rank), F32),
-        ((sweeps, nr, 2, slots * depth, rank), F32),
-        ((nr, 2, tags, rank), F32),
+        ((sweeps, 2, nr, slots * depth, rank), F32),
+        ((2, nr, tags, rank), F32),
         ((sweeps, nzc, rc, rank), F32),
         ((sweeps, nz, rc, rank), F32),
         ((sweeps, 2, nr, rank // nr // 2, rank), F32),
@@ -537,7 +476,7 @@
         ((sweeps, nr, 2, rank // nr // 2, rank), F32),
         ((sweeps, rank // nr // 2, rank), F32),
         ((sweeps, nz, rank // nr // 2, rank), F32),
-        ((sweeps, nr, 2, rank // nr // 2, rank), F32),
+        ((sweeps, 2, nr, rank // nr // 2, rank), F32),
     ]
     new_a, new_b, new_c = pl.pallas_call(
         functools.partial(kernel, nr, nc, sems),
@@ -547,12 +486,12 @@
             jax.ShapeDtypeStruct((nr, 2, nzc, rc, rank), F32),
         ),
         in_specs=[smem, smem, smem] + [far] * 4,
-        out_specs=(far, far, far),
+        out_specs=(vmem, vmem, vmem),
         scratch_shapes=[
             [pltpu.VMEM(*each) for each in one] if isinstance(one, list) else pltpu.VMEM(*one)
             for one in scratch
         ]
-        + [pltpu.SemaphoreType.DMA((4,)), pltpu.SemaphoreType.DMA((2 + 2 * nr,)), pltpu.SemaphoreType.DMA((sems,)), pltpu.SemaphoreType.DMA((sems,))],
+        + [pltpu.SemaphoreType.DMA((4,)), pltpu.SemaphoreType.DMA((sems,)), pltpu.SemaphoreType.DMA((sems,))],
         compiler_params=pltpu.CompilerParams(
             collective_id=0, has_side_effects=True, vmem_limit_bytes=VMEM_BYTES
         ),
@@ -561,7 +500,7 @@
         jnp.swapaxes(brick_coords, 2, 3), brick_counts, step_sizes,
         bricks.reshape(slots, depth, tile, tile), init_a[0], init_b[0], init_c,
     )
-    return hand_out(new_a[None], new_b[None], new_c.reshape(depth_c, rank))
+    return clamp(new_a)[None], clamp(new_b)[None], clamp(new_c.reshape(depth_c, rank))
 
 
 def solution(mesh):

time: 84.2 us -> 63.9 us (0.76)
  Pallas kernels: 82.7 us -> 59 us
  other arithmetic: 0 us -> 3.41 us
    pallas_call x1 -> x0, Pallas kernels: 21 us -> none  [hand_out(): pl.pallas_call(copy_all, out_shape=tuple((jax.ShapeDtypeStruct(one.shape,...]
    pallas_call x1, Pallas kernels: 61.8 us -> 59 us  [shards(): pl.pallas_call(functools.partial(kernel, nr, nc, sems), out_shape=(jax.Sh...]
    max x0 -> x1, other arithmetic: none -> 1.88 us  [clamp(): return jnp.maximum(values, 0.0)]
    broadcast_in_dim x0 -> x1, other arithmetic: none -> 1.53 us  [shards(): clamp(new_b)[None]]
where the time goes in v4:
time: 63.9 us; the launch traced here: 63.7 us
  Pallas kernels  59 us (92%)
  other arithmetic  3.41 us (5%)
  between operations  1.29 us (2%)
    pallas_call x1, Pallas kernels, shards(): pl.pallas_call(functools.partial(kernel, nr, nc, sems), out_shape=(jax.Sh...  59 us
    max x1, other arithmetic, clamp(): return jnp.maximum(values, 0.0)  1.88 us
    broadcast_in_dim x1, other arithmetic, shards(): clamp(new_b)[None]  1.53 us

profile of v4, /device:TPU:1, one launch (start us, length us, event | category | flops | bytes accessed | tf_op | source)
XLA Modules:
  0.0 63.7 jit_solution(14559497215963849096)
XLA Ops:
  1.3 59.0 %sweeps.1 = (f32[64,256]{1,0:T(8,128)}, f32[64,256]{1,0:T(8,128)}, f32[4,2,4,16,256]{4,3,2,1,0:T(8,128)}) custom-call(s32[1,1,2,3]{3,2,1,0:T(2,128)} %bitcast.13, s32[1,1]{1,0:T(1,128)S(6)} %copy.10.counts, f32[2,3]{1,0:T(2,128)} %rates.1, bf16[2,16,128,128]{3,2,1,0:T(8,128)(2,1)} %bitcast.9, f32[64,256]{1,0:T(8,128)} %bitcast.11, f32[64,256]{1,0:T(8,128)} %bitcast.12, ...), custom_call_target="tpu_custom_call" | custom-call | tf_op jit(solution)/shard_map/sweeps/pallas_call | solution.py:481
  60.2 1.5 %maximum_bitcast_fusion = (f32[1,64,256]{2,1,0:T(8,128)}, f32[1,64,256]{2,1,0:T(8,128)}) fusion(f32[64,256]{1,0:T(8,128)} %get-tuple-element.7, f32[64,256]{1,0:T(8,128)} %get-tuple-element.6), kind=kLoop, calls=%fused_computation.1 | loop fusion | flops 32768 | bytes 262144 | tf_op jit(solution)/shard_map/broadcast_in_dim | solution.py:503
  61.8 1.9 %broadcast_maximum_fusion = f32[4,2,4,16,256]{4,3,2,1,0:T(8,128)} fusion(f32[4,2,4,16,256]{4,3,2,1,0:T(8,128)} %get-tuple-element.8), kind=kLoop, calls=%fused_computation | loop fusion | flops 131072 | bytes 1048576 | tf_op jit(solution)/shard_map/max | solution.py:430

commit v5 on v4

--- a/solution.py
+++ b/solution.py
@@ -227,10 +227,12 @@
             )
         return to_core(da.at[s, other], da1.at[s])
 
-    def deep_stage(s):
+    def deep_stage(s, between):
         for slot in range(slots):
             fill(deep_all.at[slot], lambda k: flip[slot, k:k + batch], tile_a(s, slot))
             along_c(s, slot)
+            if slot == 0:
+                between()
         return spread_row(lambda at: cc.at[s, core, at])
 
     def drive_b_stage(s):
@@ -341,44 +343,57 @@
     for s in range(sweeps):
         last = s == sweeps - 1
         first = s == 0
-        done(far_b)
-        step_sb1 = gram_b_stage(s)
+        late = {}
+
+        def sum_b():
+            done(step_sb2)
+            sb_full[s, core, r] = total(sb2, s, nz)
+            late["sb3"] = spread_row(lambda at: sb_full.at[s, core, at])
+
+        def move_c():
+            done(far_c)
+            late["c"] = spread_row(lambda at: c_all[s].at[core, at])
+
         if first:
+            done(far_b)
+            step_sb1 = gram_b_stage(s)
             step_da1 = wide_stage(s)
-        near_a = pass_on(a_all[s].at[core], far_a)
-        step_sb2 = pair_b_stage(s, step_sb1)
-        if first:
+            near_a = pass_on(a_all[s].at[core], far_a)
+            step_sb2 = pair_b_stage(s, step_sb1)
             step_da2 = drive_a_stage(s, step_da1)
+            near_a.wait_recv()
+            step_sa1 = gram_a_stage(s)
+            step_c1 = deep_stage(s, sum_b)
+            step_db = drive_b_stage(s)
+            done(step_sa1)
+            sa_full[s, core, r] = total(sa1, s, nr)
+            step_sa2 = spread_row(lambda at: sa_full.at[s, core, at])
+            near_sb = pass_on(sb_full.at[s, core], late["sb3"])
+            near_tags = pass_on(tags.at[core], far_tags)
+            near_cc = pass_on(cc.at[s, core], step_c1)
         else:
-            done(far_c)
-            far_c = spread_row(lambda at: c_all[s].at[core, at])
-        near_a.wait_recv()
-        step_c1 = deep_stage(s)
-        step_sa1 = gram_a_stage(s)
-        if first:
-            near_tags = pass_on(tags.at[core], far_tags)
-        else:
-            near_c = pass_on(c_all[s].at[core], far_c)
-        near_cc = pass_on(cc.at[s, core], step_c1)
-        if not first:
+            near_a = pass_on(a_all[s].at[core], far_a)
+            done(far_b)
+            step_sb1 = gram_b_stage(s)
+            near_a.wait_recv()
+            step_c1 = deep_stage(s, move_c)
+            step_sb2 = pair_b_stage(s, step_sb1)
+            step_sa1 = gram_a_stage(s)
+            near_c = pass_on(c_all[s].at[core], late["c"])
+            near_cc = pass_on(cc.at[s, core], step_c1)
+            done(step_sa1)
+            sa_full[s, core, r] = total(sa1, s, nr)
+            step_sa2 = spread_row(lambda at: sa_full.at[s, core, at])
             near_c.wait_recv()
             step_da1 = wide_stage(s)
-        done(step_sa1)
-        sa_full[s, core, r] = total(sa1, s, nr)
-        step_sa2 = spread_row(lambda at: sa_full.at[s, core, at])
-        done(step_sb2)
-        sb_full[s, core, r] = total(sb2, s, nz)
-        step_sb3 = spread_row(lambda at: sb_full.at[s, core, at])
-        if first:
-            near_tags.wait_recv()
-        near_cc.wait_recv()
-        step_c3 = drive_c_stage(s)
-        if not first:
+            near_cc.wait_recv()
+            step_c3 = drive_c_stage(s)
+            sum_b()
             step_da2 = drive_a_stage(s, step_da1)
             gram_c = gram(c_all[s][...].reshape(nr * k_row, rank))
-        step_db = drive_b_stage(s)
-        near_sa = pass_on(sa_full.at[s, core], step_sa2)
-        near_sb = pass_on(sb_full.at[s, core], step_sb3)
+            near_sa = pass_on(sa_full.at[s, core], step_sa2)
+            step_db = drive_b_stage(s)
+            near_sb = pass_on(sb_full.at[s, core], late["sb3"])
         near_sb.wait_recv()
         gram_b = jnp.stack([sb_full[s, side] for side in range(2)], axis=1).reshape(rank, rank)
         if not last:
@@ -387,6 +402,10 @@
             state_a = jnp.maximum(finish(state_a, ready_a, total(da2, s, nz), rates[s, 0]), 0.0)
             a_all[s + 1][core, z] = state_a.astype(BF16)
             far_a = send_a(s + 1)
+            near_sa = pass_on(sa_full.at[s, core], step_sa2)
+            near_tags.wait_recv()
+            near_cc.wait_recv()
+            step_c3 = drive_c_stage(s)
             near_sa.wait_recv()
             gram_a = sa_full[s].reshape(rank, rank)
             ready_b = prepare(state_b, gram_a * gram_c)

time: 63.9 us -> 66 us (1.033)
  Pallas kernels: 59 us -> 61 us
    pallas_call x1, Pallas kernels: 59 us -> 61 us  [shards(): pl.pallas_call(functools.partial(kernel, nr, nc, sems), out_shape=(jax.Sh...]
where the time goes in v5:
time: 66 us; the launch traced here: 65.7 us
  Pallas kernels  61 us (92%)
  other arithmetic  3.41 us (5%)
  between operations  1.29 us (2%)
    pallas_call x1, Pallas kernels, shards(): pl.pallas_call(functools.partial(kernel, nr, nc, sems), out_shape=(jax.Sh...  61 us
    max x1, other arithmetic, clamp(): return jnp.maximum(values, 0.0)  1.88 us
    broadcast_in_dim x1, other arithmetic, shards(): clamp(new_b)[None]  1.53 us

profile of v5, /device:TPU:1, one launch (start us, length us, event | category | flops | bytes accessed | tf_op | source)
XLA Modules:
  0.0 65.7 jit_solution(8347386107958412716)
XLA Ops:
  1.3 61.0 %sweeps.1 = (f32[64,256]{1,0:T(8,128)}, f32[64,256]{1,0:T(8,128)}, f32[4,2,4,16,256]{4,3,2,1,0:T(8,128)}) custom-call(s32[1,1,2,3]{3,2,1,0:T(2,128)} %bitcast.13, s32[1,1]{1,0:T(1,128)S(6)} %copy.10.counts, f32[2,3]{1,0:T(2,128)} %rates.1, bf16[2,16,128,128]{3,2,1,0:T(8,128)(2,1)} %bitcast.9, f32[64,256]{1,0:T(8,128)} %bitcast.11, f32[64,256]{1,0:T(8,128)} %bitcast.12, ...), custom_call_target="tpu_custom_call" | custom-call | tf_op jit(solution)/shard_map/sweeps/pallas_call | solution.py:500
  62.3 1.5 %maximum_bitcast_fusion = (f32[1,64,256]{2,1,0:T(8,128)}, f32[1,64,256]{2,1,0:T(8,128)}) fusion(f32[64,256]{1,0:T(8,128)} %get-tuple-element.7, f32[64,256]{1,0:T(8,128)} %get-tuple-element.6), kind=kLoop, calls=%fused_computation.1 | loop fusion | flops 32768 | bytes 262144 | tf_op jit(solution)/shard_map/broadcast_in_dim | solution.py:522
  63.9 1.9 %broadcast_maximum_fusion = f32[4,2,4,16,256]{4,3,2,1,0:T(8,128)} fusion(f32[4,2,4,16,256]{4,3,2,1,0:T(8,128)} %get-tuple-element.8), kind=kLoop, calls=%fused_computation | loop fusion | flops 131072 | bytes 1048576 | tf_op jit(solution)/shard_map/max | solution.py:449

commit v6 on v4

--- a/solution.py
+++ b/solution.py
@@ -356,6 +356,7 @@
         step_c1 = deep_stage(s)
         step_sa1 = gram_a_stage(s)
         if first:
+            step_db = drive_b_stage(s)
             near_tags = pass_on(tags.at[core], far_tags)
         else:
             near_c = pass_on(c_all[s].at[core], far_c)
@@ -376,7 +377,7 @@
         if not first:
             step_da2 = drive_a_stage(s, step_da1)
             gram_c = gram(c_all[s][...].reshape(nr * k_row, rank))
-        step_db = drive_b_stage(s)
+            step_db = drive_b_stage(s)
         near_sa = pass_on(sa_full.at[s, core], step_sa2)
         near_sb = pass_on(sb_full.at[s, core], step_sb3)
         near_sb.wait_recv()
@@ -426,8 +427,36 @@
     assert used[0] <= sems_of
 
 
-def clamp(values):
-    return jnp.maximum(values, 0.0)
+def clamp(*arrays):
+    count = len(arrays)
+
+    def clamp_all(*refs):
+        inner, outer, held, sems = refs[:count], refs[count:2 * count], refs[2 * count:-1], refs[-1]
+        loads = [
+            pltpu.make_async_copy(inner[at], held[at], sems.at[at]) for at in range(count)
+        ]
+        for load in loads:
+            load.start()
+        copies = []
+        for at in range(count):
+            loads[at].wait()
+            held[at][...] = jnp.maximum(held[at][...], 0.0)
+            copies.append(pltpu.make_async_copy(held[at], outer[at], sems.at[count + at]))
+            copies[-1].start()
+        for copy in copies:
+            copy.wait()
+
+    far = pl.BlockSpec(memory_space=pltpu.HBM)
+    return pl.pallas_call(
+        clamp_all,
+        out_shape=tuple(jax.ShapeDtypeStruct(one.shape, one.dtype) for one in arrays),
+        in_specs=[far] * count,
+        out_specs=(far,) * count,
+        scratch_shapes=[pltpu.VMEM(one.shape, one.dtype) for one in arrays]
+        + [pltpu.SemaphoreType.DMA((2 * count,))],
+        compiler_params=pltpu.CompilerParams(vmem_limit_bytes=VMEM_BYTES),
+        name="clamp",
+    )(*arrays)
 
 
 def shards(nr, nc, bricks, brick_coords, brick_counts, step_sizes, init_a, init_b, init_c):
@@ -500,7 +529,8 @@
         jnp.swapaxes(brick_coords, 2, 3), brick_counts, step_sizes,
         bricks.reshape(slots, depth, tile, tile), init_a[0], init_b[0], init_c,
     )
-    return clamp(new_a)[None], clamp(new_b)[None], clamp(new_c.reshape(depth_c, rank))
+    last_a, last_b, last_c = clamp(new_a, new_b, new_c.reshape(depth_c, rank))
+    return last_a[None], last_b[None], last_c
 
 
 def solution(mesh):

time: 63.9 us -> 61.9 us (0.969)
  other arithmetic: 3.41 us -> 0 us
  Pallas kernels: 59 us -> 60.4 us
    pallas_call x0 -> x1, Pallas kernels: none -> 2 us  [clamp(): pl.pallas_call(clamp_all, out_shape=tuple((jax.ShapeDtypeStruct(one.shape...]
    max x1 -> x0, other arithmetic: 1.88 us -> none  [clamp(): return jnp.maximum(values, 0.0)]
    broadcast_in_dim x1 -> x0, other arithmetic: 1.53 us -> none  [shards(): clamp(new_b)[None]]
where the time goes in v6:
time: 61.9 us; the launch traced here: 61.7 us
  Pallas kernels  60.4 us (98%)
  between operations  1.29 us (2%)
    pallas_call x1, Pallas kernels, shards(): pl.pallas_call(functools.partial(kernel, nr, nc, sems), out_shape=(jax.Sh...  58.4 us
    pallas_call x1, Pallas kernels, clamp(): pl.pallas_call(clamp_all, out_shape=tuple((jax.ShapeDtypeStruct(one.shape...  2 us

profile of v6, /device:TPU:1, one launch (start us, length us, event | category | flops | bytes accessed | tf_op | source)
XLA Modules:
  0.0 61.7 jit_solution(17290799822530792241)
XLA Ops:
  1.3 58.4 %sweeps.1 = (f32[64,256]{1,0:T(8,128)}, f32[64,256]{1,0:T(8,128)}, f32[4,2,4,16,256]{4,3,2,1,0:T(8,128)}) custom-call(s32[1,1,2,3]{3,2,1,0:T(2,128)} %bitcast.11, s32[1,1]{1,0:T(1,128)S(6)} %copy.10.counts, f32[2,3]{1,0:T(2,128)} %rates.1, bf16[2,16,128,128]{3,2,1,0:T(8,128)(2,1)} %bitcast.7, f32[64,256]{1,0:T(8,128)} %bitcast.9, f32[64,256]{1,0:T(8,128)} %bitcast.10, ...), custom_call_target="tpu_custom_call" | custom-call | tf_op jit(solution)/shard_map/sweeps/pallas_call | solution.py:510
  59.7 2.0 %clamp.1 = (f32[64,256]{1,0:T(8,128)}, f32[64,256]{1,0:T(8,128)}, f32[512,256]{1,0:T(8,128)}) custom-call(f32[64,256]{1,0:T(8,128)} %get-tuple-element.9.refs_0_, f32[64,256]{1,0:T(8,128)} %get-tuple-element.10.refs_1_, f32[512,256]{1,0:T(8,128)} %bitcast.8), custom_call_target="tpu_custom_call" | custom-call | tf_op jit(solution)/shard_map/clamp/pallas_call | solution.py:450
